TPU v7x, 256 devices: a whole 4x4x8 slice. The times are simulated.
256 devices in a mesh: context: 32 (over x, y, core), tensor: 8 (over z).
Axes of the slice: x: 4, y: 4, z: 8, core: 2. Of those that a mesh axis runs over, the one named last changes fastest.
Arguments:
- inner_in: bfloat16 [4096, 8192], P('context', 'tensor'), may hold values from -6 to 6
- gate_in: bfloat16 [4096, 8192], P('context', 'tensor'), may hold values from -6 to 6
- out_grad: bfloat16 [4096, 8192], P('context', 'tensor'), may hold values from -6 to 6
- kernel: float32 [8192, 4], P('tensor'), may hold values from -3 to 3
- kernel_shift: float32 [8192], P('tensor'), may hold values from -0.5 to 0.5
- select_proj: bfloat16 [544, 8192], P(None, 'tensor'), may hold values from -0.0625 to 0.0625
- delta_proj: bfloat16 [8192, 512], P('tensor'), may hold values from -0.25 to 0.25
- delta_bias: float32 [8192], P('tensor'), may hold values from -7 to -2
- decay_log: float32 [8192, 16], P('tensor'), may hold values from -1 to 2.8
- skip_gain: float32 [8192], P('tensor'), may hold values from 0.5 to 1.5
Outputs:
- inner_grad: bfloat16 [4096, 8192], P('context', 'tensor')
- gate_grad: bfloat16 [4096, 8192], P('context', 'tensor')
- kernel_grad: float32 [8192, 4], P('tensor')
- shift_grad: float32 [8192], P('tensor')
- select_grad: float32 [544, 8192], P('context', 'tensor')
- delta_grad: float32 [8192, 512], P('tensor', 'context')
- bias_grad: float32 [8192], P('tensor')
- decay_grad: float32 [8192, 16], P('tensor')
- skip_grad: float32 [8192], P('tensor')
All inputs are finite; a program needn't handle non-finite values.
Results may differ from a plain program's by a relative error of at most 0.017.
Values may be sent and summed in bfloat16 or wider, within the bound.
A program may use at most 128 MiB of HBM per device.

v0:
```python
import jax
import jax.numpy as jnp
from jax import lax
from jax.sharding import PartitionSpec as P

N_STATE = 16
RANK = 512
KCONV = 4
BLOCK = 32


def passed_along(value, axis, steps):
    count = lax.axis_size(axis)
    leading, last = (max(0, -steps), min(count, count - steps))
    return lax.ppermute(value, axis, [(source, source + steps) for source in range(leading, last)])


def silu_slope(values):
    logistic = jax.nn.sigmoid(values)
    return logistic * (1.0 + values * (1.0 - logistic))


def combine(first, second):
    return (first[0] * second[0], second[0] * first[1] + second[1])


def scan_pairs(decays, additions, backward):
    return lax.associative_scan(combine, (decays, additions), axis=0, reverse=backward)


def body(
    inner_in,
    gate_in,
    out_grad,
    kernel,
    kernel_shift,
    select_proj,
    delta_proj,
    delta_bias,
    decay_log,
    skip_gain,
):
    rows = inner_in.shape[0]
    breadth = inner_in.shape[1]
    groups = rows // BLOCK
    halo_rows = passed_along(inner_in[rows - (KCONV - 1) :], "context", 1)
    padded = jnp.concatenate([halo_rows, inner_in], 0).astype(jnp.float32)
    conv_pre = jnp.zeros((rows, breadth), jnp.float32) + kernel_shift[None, :]
    for position in range(KCONV):
        conv_pre = conv_pre + kernel[:, position][None, :] * padded[position : position + rows]
    conv_out = jax.nn.silu(conv_pre)
    conv_half = conv_out.astype(jnp.bfloat16)
    partial_proj = jnp.dot(conv_half, select_proj.T, preferred_element_type=jnp.float32)
    projected = lax.psum(partial_proj, "tensor")
    low_rank = projected[:, :RANK].astype(jnp.bfloat16)
    input_mat = projected[:, RANK : RANK + N_STATE]
    output_mat = projected[:, RANK + N_STATE :]
    delta_raw = (
        jnp.dot(low_rank, delta_proj.T, preferred_element_type=jnp.float32) + delta_bias[None, :]
    )
    deltas = jax.nn.softplus(delta_raw)
    decay_rate = -jnp.exp(decay_log).T
    gate_value = gate_in.astype(jnp.float32)
    out_cot = out_grad.astype(jnp.float32) * jax.nn.silu(gate_value)
    unit = jnp.ones((N_STATE, breadth), jnp.float32)
    empty = jnp.zeros((N_STATE, breadth), jnp.float32)

    def blocked(array):
        return array.reshape((groups, BLOCK) + array.shape[1:])

    sectioned = (
        blocked(conv_out),
        blocked(deltas),
        blocked(out_cot),
        blocked(input_mat),
        blocked(output_mat),
    )

    def prepare(conv_part, delta_part, cot_part, input_part, output_part):
        decays = jnp.exp(delta_part[:, None, :] * decay_rate[None])
        inflow = (delta_part * conv_part)[:, None, :] * input_part[:, :, None]
        source = output_part[:, :, None] * cot_part[:, None, :]
        follow = jnp.concatenate([decays[1:], unit[None]], 0)
        return (decays, inflow, source, follow)

    def summarize(pieces):
        conv_part, delta_part, cot_part, input_part, output_part = pieces
        log_decay = delta_part[:, None, :] * decay_rate[None]
        prefix = jnp.cumsum(log_decay, axis=0)
        total = prefix[-1]
        inflow = (delta_part * conv_part)[:, None, :] * input_part[:, :, None]
        source = output_part[:, :, None] * cot_part[:, None, :]
        ending = jnp.sum(inflow * jnp.exp(total[None] - prefix), axis=0)
        outflow = jnp.sum(source * jnp.exp(prefix), axis=0)
        return (jnp.exp(total), ending, outflow)

    products, endings, outflows = lax.map(summarize, sectioned)

    def fold(carried, element):
        return (combine(carried, element), None)

    (device_decay, device_state), _ = lax.scan(fold, (unit, empty), (products, endings))
    (_, device_outflow), _ = lax.scan(fold, (unit, empty), (products, outflows), reverse=True)

    def relay(position, carried):
        incoming_now, returning_now = carried
        incoming_now = passed_along(device_decay * incoming_now + device_state, "context", 1)
        returning_now = passed_along(device_decay * returning_now + device_outflow, "context", -1)
        return (incoming_now, returning_now)

    incoming, returning = lax.fori_loop(0, lax.axis_size("context") - 1, relay, (empty, empty))

    def advance(carried, element):
        return (element[0] * carried + element[1], carried)

    _, starts = lax.scan(advance, incoming, (products, endings))
    _, afters = lax.scan(advance, returning, (products, outflows), reverse=True)

    def gradients(rate_sum, pieces):
        conv_part, delta_part, cot_part, input_part, output_part, start_state, after_state = pieces
        decays, inflow, source, follow = prepare(
            conv_part, delta_part, cot_part, input_part, output_part
        )
        inflow = jnp.concatenate([inflow[:1] + decays[:1] * start_state[None], inflow[1:]], 0)
        source = jnp.concatenate([source[:-1], source[-1:] + after_state[None]], 0)
        _, states = scan_pairs(decays, inflow, False)
        _, adjoint = scan_pairs(follow, source, True)
        earlier = jnp.concatenate([start_state[None], states[:-1]], 0)
        outputs = jnp.einsum("tnc,tn->tc", states, output_part) + skip_gain[None, :] * conv_part
        along_input = jnp.einsum("tnc,tn->tc", adjoint, input_part)
        direct = skip_gain[None, :] * cot_part + delta_part * along_input
        weighted = adjoint * decays * earlier
        delta_cot = jnp.sum(weighted * decay_rate[None], axis=1) + conv_part * along_input
        input_cot = jnp.einsum("tnc,tc->tn", adjoint, delta_part * conv_part)
        output_cot = jnp.einsum("tnc,tc->tn", states, cot_part)
        rate_cot = jnp.sum(weighted * delta_part[:, None, :], axis=0)
        return (rate_sum + rate_cot, (outputs, direct, delta_cot, input_cot, output_cot))

    rate_total, results = lax.scan(gradients, empty, sectioned + (starts, afters))
    outputs = results[0].reshape(rows, breadth)
    direct = results[1].reshape(rows, breadth)
    delta_cot = results[2].reshape(rows, breadth)
    input_cot = results[3].reshape(rows, N_STATE)
    output_cot = results[4].reshape(rows, N_STATE)
    gate_grad = (out_grad.astype(jnp.float32) * outputs * silu_slope(gate_value)).astype(
        jnp.bfloat16
    )
    raw_cot = delta_cot * jax.nn.sigmoid(delta_raw)
    raw_half = raw_cot.astype(jnp.bfloat16)
    rank_part = jnp.dot(raw_half, delta_proj, preferred_element_type=jnp.float32)
    select_sum = lax.psum(jnp.concatenate([rank_part, input_cot, output_cot], 1), "tensor")
    select_cot = select_sum.astype(jnp.bfloat16)
    conv_cot = direct + jnp.dot(select_cot, select_proj, preferred_element_type=jnp.float32)
    pre_cot = conv_cot * silu_slope(conv_pre)
    below = passed_along(pre_cot[: KCONV - 1], "context", -1)
    trailing = jnp.concatenate([pre_cot, below], 0)
    inner_grad = jnp.zeros((rows, breadth), jnp.float32)
    for position in range(KCONV):
        first_row = KCONV - 1 - position
        inner_grad = (
            inner_grad + kernel[:, position][None, :] * trailing[first_row : first_row + rows]
        )
    inner_grad = inner_grad.astype(jnp.bfloat16)
    select_term = jnp.dot(select_cot.T, conv_half, preferred_element_type=jnp.float32)
    delta_term = jnp.dot(low_rank.T, raw_half, preferred_element_type=jnp.float32)
    select_grad, delta_share = (
        lax.psum_scatter(select_term, "context", scatter_dimension=0, tiled=True),
        lax.psum_scatter(delta_term, "context", scatter_dimension=0, tiled=True),
    )
    delta_grad = delta_share.T
    kernel_part = jnp.stack(
        [jnp.sum(pre_cot * padded[position : position + rows], 0) for position in range(KCONV)], 1
    )
    shift_part = jnp.sum(pre_cot, 0)
    bias_part = jnp.sum(raw_cot, 0)
    decay_part = (rate_total * decay_rate).T
    skip_part = jnp.sum(out_cot * conv_out, 0)
    kernel_grad, shift_grad, bias_grad, decay_grad, skip_grad = lax.psum(
        (kernel_part, shift_part, bias_part, decay_part, skip_part), "context"
    )
    return (
        inner_grad,
        gate_grad,
        kernel_grad,
        shift_grad,
        select_grad,
        delta_grad,
        bias_grad,
        decay_grad,
        skip_grad,
    )


def solution(mesh):
    return jax.shard_map(
        body,
        mesh=mesh,
        in_specs=(
            P("context", "tensor"),
            P("context", "tensor"),
            P("context", "tensor"),
            P("tensor", None),
            P("tensor"),
            P(None, "tensor"),
            P("tensor", None),
            P("tensor"),
            P("tensor", None),
            P("tensor"),
        ),
        out_specs=(
            P("context", "tensor"),
            P("context", "tensor"),
            P("tensor", None),
            P("tensor"),
            P("context", "tensor"),
            P("tensor", "context"),
            P("tensor"),
            P("tensor", None),
            P("tensor"),
        ),
        check_vma=False,
    )
```

profile of v0, /device:TPU:1, one launch (start us, length us, event | category | flops | bytes accessed | tf_op | source)
XLA Modules:
  0.0 1401.8 jit_solution(4267430819265790086)
XLA Ops:
  22.0 69.5 %all-reduce.28.cloned.1.call-done = f32[128,544]{0,1:T(8,128)} async-done(((f32[128,544]{0,1:T(8,128)}), f32[128,544]{0,1:T(8,128)}) %all-reduce.28.cloned.1.call-update) | async-done | bytes 278544 | tf_op jit(solution)/shard_map/psum | solution.py:54
  98.4 35.3 %while.103 = (s32[]{:T(128)}, f32[4,16,1024]{2,1,0:T(8,128)}, f32[4,16,1024]{2,1,0:T(8,128)}, f32[4,16,1024]{2,1,0:T(8,128)}, f32[4,32,1024]{2,1,0:T(8,128)}, /*...) while((s32[]{:T(128)}, f32[4,16,1024]{2,1,0:T(8,128)}, ...), condition=%wide.region_5.6_spmd, body=%wide.region_1.5_spmd.sunk | while | flops 20447232 | bytes 6243965 | solution.py:97
  133.8 6.2 while.108
  139.9 6.4 while.107
  146.4 324.9 %while.104 = (s32[]{:T(128)}, f32[16,1024]{1,0:T(8,128)S(1)}, f32[16,1024]{1,0:T(8,128)S(1)}, f32[16,1024]{1,0:T(8,128)}, f32[16,1024]{1,0:T(8,128)}, /*index=5*/f32[16,1024]{1,0:T(8,128)S(1)}, s32[]{:T(128)}) while((s32[]{:T(128)}, f32[16,1024]{1,0:T(8,128)S(1)}, f32[16,1024]{1,0:T(8,128)S(1)}, f32[16,1024]{1,0:T(8,128)}, ...), condition=%wide.region_11.12_spmd, body=%wide.region_10.11_spmd.sunk | while | flops 65538 | bytes 983197 | solution.py:111
  147.3 7.9 collective-permute-start
  266.2 5.3 collective-permute-done.1
  472.0 6.0 while.106
  478.7 6.1 while.105
  484.8 631.5 %while.109 = (s32[]{:T(128)}, f32[16,1024]{1,0:T(8,128)}, f32[4,32,1024]{2,1,0:T(8,128)}, f32[4,32,1024]{2,1,0:T(8,128)}, f32[4,32,1024]{2,1,0:T(8,128)}, /*inde...) while((s32[]{:T(128)}, f32[16,1024]{1,0:T(8,128)}, ...), condition=%wide.region_19.20_spmd.clone, body=%wide.region_16.19_spmd.clone.sunk | while | flops 20889604 | bytes 238060208 | solution.py:139
  513.2 5.7 pad.297
  521.0 5.7 pad.296
  529.4 10.1 pad.299
  544.1 10.2 pad.298
  590.3 5.7 pad.289
  599.2 5.7 pad.288
  608.2 7.0 pad.291
  617.9 10.1 pad.290
  671.0 5.7 pad.297
  678.8 5.7 pad.296
  687.3 10.1 pad.299
  702.0 10.2 pad.298
  748.1 5.7 pad.289
  757.1 5.7 pad.288
  766.1 7.0 pad.291
  775.8 10.1 pad.290
  828.9 5.7 pad.297
  836.7 5.7 pad.296
  845.1 10.1 pad.299
  859.9 10.2 pad.298
  906.0 5.7 pad.289
  915.0 5.7 pad.288
  924.0 7.0 pad.291
  933.6 10.1 pad.290
  986.8 5.7 pad.297
  994.6 5.7 pad.296
  1003.0 10.1 pad.299
  1017.7 10.2 pad.298
  1063.9 5.7 pad.289
  1072.8 5.7 pad.288
  1081.8 7.0 pad.291
  1091.5 10.1 pad.290
  1122.1 26.2 %all-reduce.31 = bf16[128,544]{1,0:T(8,128)(2,1)S(1)} all-reduce(f32[128,544]{1,0:T(8,128)S(1)} %pad_maximum_fusion.11), channel_id=1, replica_groups=mesh['context'=32,'tensor'=8] {'tensor'}, use_global_device_ids=true, to_apply=%region_20.21 | all-reduce | flops 69632 | bytes 417792 | tf_op jit(solution)/shard_map/psum | solution.py:151
  1149.9 76.0 %fusion = f32[24,1024]{1,0:T(8,128)} fusion(f32[544,1024]{1,0:T(8,128)S(1)} %fusion.51), kind=kCustom, calls=%all-reduce-scatter | all-reduce-scatter fusion | flops 786433 | bytes 2327552
  1226.0 5.4 collective-permute-start.10
  1251.8 8.1 collective-permute-start.6
  1261.3 6.0 collective-permute-start.8
  1272.6 119.0 %all-reduce.23 = (f32[1024,4]{0,1:T(4,128)}, f32[1024]{0:T(1024)}, f32[1024]{0:T(1024)}, f32[1024]{0:T(1024)}) all-reduce(f32[1024,4]{0,1:T(4,128)S(1)} %pad_maximum_fusion.12, f32[1024]{0:T(1024)S(1)} %get-tuple-element.611, f32[1024]{0:T(1024)S(1)} %get-tuple-element.722, ...), channel_id=1, replica_groups=mesh['context'=32,'tensor'=8] {'context'}, use_global_device_ids=true, to_apply=%region_25.26 | all-reduce | flops 7168 | bytes 57344 | tf_op jit(solution)/shard_map/psum | solution.py:178
  (933 shorter events, 819.3 us)
Async XLA Ops:
  7.2 84.4 %all-reduce.28.cloned.1.call-start = ((), (), s32[]{:S(2)}) async-start(), calls=%async_computation.1 | async-start | bytes 557056 | tf_op jit(solution)/shard_map/psum | solution.py:54
  8.0 5.5 collective-permute-start.2
  19.7 1374.1 %all-reduce.30.cloned.1.call-start = ((), (), s32[]{:S(2)}) async-start(), calls=%async_computation.3 | async-start | bytes 131072 | tf_op jit(solution)/shard_map/psum | solution.py:178
  147.3 9.9 collective-permute-start
  155.2 5.6 collective-permute-start.1
  161.7 4.3 collective-permute-start
  163.6 5.6 collective-permute-start.1
  170.1 4.3 collective-permute-start
  172.0 5.6 collective-permute-start.1
  180.4 6.9 collective-permute-start.1
  190.1 7.7 collective-permute-start.1
  200.7 7.7 collective-permute-start.1
  211.2 7.7 collective-permute-start.1
  221.7 7.7 collective-permute-start.1
  232.2 7.7 collective-permute-start.1
  242.7 7.7 collective-permute-start.1
  253.2 7.7 collective-permute-start.1
  263.7 7.7 collective-permute-start.1
  274.3 7.7 collective-permute-start.1
  284.8 7.7 collective-permute-start.1
  295.3 7.7 collective-permute-start.1
  305.8 7.7 collective-permute-start.1
  316.3 7.7 collective-permute-start.1
  326.8 7.7 collective-permute-start.1
  337.4 7.7 collective-permute-start.1
  347.9 7.7 collective-permute-start.1
  358.4 7.7 collective-permute-start.1
  368.9 7.7 collective-permute-start.1
  379.4 7.7 collective-permute-start.1
  389.9 7.7 collective-permute-start.1
  400.5 7.7 collective-permute-start.1
  411.0 7.7 collective-permute-start.1
  421.5 7.7 collective-permute-start.1
  432.0 7.7 collective-permute-start.1
  442.5 7.7 collective-permute-start.1
  453.0 7.7 collective-permute-start.1
  463.5 7.7 collective-permute-start.1
  1120.2 273.6 %reduce-scatter.4.cloned.1.call-start = ((), (), s32[]{:S(2)}) async-start(), calls=%async_computation.2 | async-start | bytes 2162688 | tf_op jit(solution)/shard_map/reduce_scatter | solution.py:168
  1226.0 25.8 %collective-permute-start.10 = (f32[24,1024]{1,0:T(8,128)}, f32[24,1024]{1,0:T(8,128)S(1)}, u32[]{:S(2)}, u32[]{:S(2)}) collective-permute-start(f32[24,1024]{1,0:T(8,128)} %fusion), channel_id=1, source_target_pairs={{0,56},{8,64},{16,72},{24,80},{32,88},{40,96},{48,104},{56,112},{6... | collective-permute-start | bytes 294920
  1231.4 28.5 %collective-permute-start.11 = (f32[24,1024]{1,0:T(8,128)}, f32[24,1024]{1,0:T(8,128)S(1)}, u32[]{:S(2)}, u32[]{:S(2)}) collective-permute-start(f32[24,1024]{1,0:T(8,128)} %fusion), channel_id=1, source_target_pairs={{0,64},{8,72},{16,80},{24,88},{32,96},{40,104},{48,112},{56,120},{... | collective-permute-start | bytes 294920
  1234.4 26.8 %collective-permute-start.12 = (f32[24,1024]{1,0:T(8,128)}, f32[24,1024]{1,0:T(8,128)S(1)}, u32[]{:S(2)}, u32[]{:S(2)}) collective-permute-start(f32[24,1024]{1,0:T(8,128)} %fusion), channel_id=1, source_target_pairs={{0,72},{8,80},{16,88},{24,96},{32,104},{40,112},{48,120},{56,128},... | collective-permute-start | bytes 294920
  1237.1 30.2 %collective-permute-start.4 = (f32[24,1024]{1,0:T(8,128)}, f32[24,1024]{1,0:T(8,128)S(1)}, u32[]{:S(2)}, u32[]{:S(2)}) collective-permute-start(f32[24,1024]{1,0:T(8,128)} %fusion), channel_id=1, source_target_pairs={{0,8},{8,16},{16,24},{24,32},{32,40},{40,48},{48,56},{56,64},{64,7... | collective-permute-start | bytes 294920
  1240.7 5.1 collective-permute-start.3
  1248.3 143.2 %collective-permute-start.5 = (f32[24,1024]{1,0:T(8,128)S(1)}, f32[24,1024]{1,0:T(8,128)S(1)}, u32[]{:S(2)}, u32[]{:S(2)}) collective-permute-start(f32[24,1024]{1,0:T(8,128)S(1)} %copy-done.44), channel_id=1, source_target_pairs={{0,16},{8,24},{16,32},{24,40},{32,48},{40,56},{48,64},{56,72},{64,... | collective-permute-start | bytes 294920
  1251.8 139.7 %collective-permute-start.6 = (f32[24,1024]{1,0:T(8,128)S(1)}, f32[24,1024]{1,0:T(8,128)S(1)}, u32[]{:S(2)}, u32[]{:S(2)}) collective-permute-start(f32[24,1024]{1,0:T(8,128)S(1)} %copy-done.44), channel_id=1, source_target_pairs={{0,24},{8,32},{16,40},{24,48},{32,56},{40,64},{48,72},{56,80},{64,... | collective-permute-start | bytes 294920
  1259.9 131.6 %collective-permute-start.7 = (f32[24,1024]{1,0:T(8,128)S(1)}, f32[24,1024]{1,0:T(8,128)S(1)}, u32[]{:S(2)}, u32[]{:S(2)}) collective-permute-start(f32[24,1024]{1,0:T(8,128)S(1)} %copy-done.44), channel_id=1, source_target_pairs={{0,32},{8,40},{16,48},{24,56},{32,64},{40,72},{48,80},{56,88},{64,... | collective-permute-start | bytes 294920
  1261.3 130.3 %collective-permute-start.8 = (f32[24,1024]{1,0:T(8,128)S(1)}, f32[24,1024]{1,0:T(8,128)S(1)}, u32[]{:S(2)}, u32[]{:S(2)}) collective-permute-start(f32[24,1024]{1,0:T(8,128)S(1)} %copy-done.44), channel_id=1, source_target_pairs={{0,40},{8,48},{16,56},{24,64},{32,72},{40,80},{48,88},{56,96},{64,... | collective-permute-start | bytes 294920
  1267.3 124.3 %collective-permute-start.9 = (f32[24,1024]{1,0:T(8,128)S(1)}, f32[24,1024]{1,0:T(8,128)S(1)}, u32[]{:S(2)}, u32[]{:S(2)}) collective-permute-start(f32[24,1024]{1,0:T(8,128)S(1)} %copy-done.44), channel_id=1, source_target_pairs={{0,48},{8,56},{16,64},{24,72},{32,80},{40,88},{48,96},{56,104},{64... | collective-permute-start | bytes 294920
  (186 other events, 1008.2 us)
Sparse Core Ops, SparseCore 0:
  19.8 71.7 all-reduce.27
  1120.3 110.8 all-reduce.29
  1235.6 83.4 reduce-scatter.3
where the time goes:
time: 1430 us; the launch traced here: 1400 us
  local copies, waits for them, and re-layouts  455 us (32%)
  other arithmetic  258 us (18%)
  waiting for transfers between devices  228 us (16%)
  blocking collectives  221 us (15%)
  starting transfers between devices  185 us (13%)
  matrix products  37.2 us (3%)
  between operations  15.1 us (1%)
    pad x64, local copies, waits for them, and re-layouts, scan_pairs(): lax.associative_scan(combine, (decays, additions), axis=0, reverse=backward)  319 us
    ppermute x64, waiting for transfers between devices, passed_along(): lax.ppermute(value, axis, [(source, source + steps) for source in range(l...  158 us
    ppermute x64, starting transfers between devices, passed_along(): lax.ppermute(value, axis, [(source, source + steps) for source in range(l...  147 us
    psum x1, blocking collectives, body(): lax.psum((kernel_part, shift_part, bias_part, decay_part, skip_part), 'co...  119 us
    add x40, other arithmetic, scan_pairs(): lax.associative_scan(combine, (decays, additions), axis=0, reverse=backward)  85.6 us
    unnamed x1, blocking collectives  76 us
    psum x1, waiting for transfers between devices, body(): projected = lax.psum(partial_proj, 'tensor')  69.5 us
    add x36, other arithmetic, combine(): return (first[0] * second[0], second[0] * first[1] + second[1])  45 us
  transfers between devices with their start and end apart: 77, of which 33 were waited for; matrix products, arithmetic and copies ran while one was open for 6% of the time, Pallas kernels for 0%

commit v1 on v0

v1 whole, which is shorter than its diff:
```python
import functools

import jax
import jax.numpy as jnp
from jax import lax
from jax.experimental import pallas as pl
from jax.experimental.pallas import tpu as pltpu
from jax.sharding import PartitionSpec as P

N = 16
RANK = 512
TAPS = 4
PROJ = 544
WIDE = 640
T = 128
C = 1024
H = 512
CTX = 32
TEN = 8
ROWS = T // TEN
LOG2E = 1.4426950408889634
MESH = pl.DeviceIdType.MESH
F32 = jnp.float32
BF16 = jnp.bfloat16
VMEM = pl.BlockSpec(memory_space=pltpu.VMEM)


def dot_nn(a, b):
    return lax.dot_general(a, b, (((1,), (0,)), ((), ())), preferred_element_type=F32)


def dot_nt(a, b):
    return lax.dot_general(a, b, (((1,), (1,)), ((), ())), preferred_element_type=F32)


def dot_tn(a, b):
    return lax.dot_general(a, b, (((0,), (0,)), ((), ())), preferred_element_type=F32)


def iota(shape, axis):
    return lax.broadcasted_iota(jnp.int32, shape, axis)


def sigmoid(v):
    return jax.nn.sigmoid(v)


def silu_slope(v):
    s = sigmoid(v)
    return s * (1.0 + v * (1.0 - s))


def split_tile(v):
    high = v.astype(BF16).astype(F32)
    return jnp.where(iota(v.shape, 1) < 64, high, v - high).astype(BF16)


class Exchange:
    def __init__(self, src, dst, send, recv, axis, size, same=False):
        self.src, self.dst, self.send, self.recv = src, dst, send, recv
        self.axis, self.size, self.same = axis, size, same

    def copy(self, off):
        me = lax.axis_index(self.axis)
        peer = lax.rem(me + off, self.size)
        return pltpu.make_async_remote_copy(
            src_ref=self.src.at[me] if self.same else self.src.at[peer],
            dst_ref=self.dst.at[me],
            send_sem=self.send.at[off],
            recv_sem=self.recv.at[off],
            device_id={self.axis: peer},
            device_id_type=MESH,
        )

    def start(self):
        lax.fori_loop(1, self.size, lambda off, _: (self.copy(off).start(), 0)[1], 0)

    def wait_recv(self):
        lax.fori_loop(1, self.size, lambda off, _: (self.copy(off).wait_recv(), 0)[1], 0)

    def wait_send(self):
        lax.fori_loop(1, self.size, lambda off, _: (self.copy(off).wait_send(), 0)[1], 0)


def greet(axis, size):
    me = lax.axis_index(axis)
    barrier = pltpu.get_barrier_semaphore()

    def signal(off, _):
        pl.semaphore_signal(
            barrier, inc=1, device_id={axis: lax.rem(me + off, size)}, device_id_type=MESH
        )
        return 0

    lax.fori_loop(1, size, signal, 0)


def to_neighbour(src, dst, send, recv, step):
    peer = lax.rem(lax.axis_index("context") + step + CTX, CTX)
    return pltpu.make_async_remote_copy(
        src_ref=src, dst_ref=dst, send_sem=send, recv_sem=recv,
        device_id={"context": peer}, device_id_type=MESH,
    )


def front_kernel(
    inner, taps, shift, wsel, pad, pre, proj,
    halo, wtail, part, got, hs, hr, ss, sr, gs, gr,
):
    ctx, ten = lax.axis_index("context"), lax.axis_index("tensor")
    barrier = pltpu.get_barrier_semaphore()
    for step in (1, CTX - 1):
        pl.semaphore_signal(
            barrier, inc=1, device_id={"context": lax.rem(ctx + step, CTX)}, device_id_type=MESH
        )
    greet("tensor", TEN)
    pl.semaphore_wait(barrier, TEN + 1)

    edge = to_neighbour(inner.at[pl.ds(T - 16, 16)], halo, hs, hr, 1)
    edge.start()
    tail = wsel[RANK:PROJ, :]
    wtail[0:32, :] = tail
    wtail[32:64, :] = jnp.zeros((32, C), BF16)
    wtail[64:96, :] = tail
    wtail[96:128, :] = jnp.zeros((32, C), BF16)
    pad[16:, :] = inner[...].astype(F32)
    edge.wait()
    pad[0:16, :] = halo[...].astype(F32) * (ctx > 0).astype(F32)

    value = jnp.zeros((T, C), F32) + shift[...]
    for k in range(TAPS):
        value = value + taps[k : k + 1, :] * pad[pl.ds(16 - TAPS + 1 + k, T), :]
    pre[...] = value
    half = (value * sigmoid(value)).astype(BF16)
    part[:, :, :RANK] = dot_nt(half, wsel[:RANK, :]).astype(BF16).reshape(TEN, ROWS, RANK)
    part[:, :, RANK:] = split_tile(dot_nt(half, wtail[...])).reshape(TEN, ROWS, 128)

    scatter = Exchange(part, got, ss, sr, "tensor", TEN)
    scatter.start()
    got[ten] = part[ten]
    scatter.wait_recv()
    total = jnp.sum(got[...].astype(F32), axis=0)
    bc = total[:, RANK:]
    bc = bc + pltpu.roll(bc, 64, 1)
    proj[ten, :, :RANK] = total[:, :RANK].astype(BF16)
    proj[ten, :, RANK:] = split_tile(bc)
    gather = Exchange(proj, proj, gs, gr, "tensor", TEN, same=True)
    gather.start()
    gather.wait_recv()
    scatter.wait_send()
    gather.wait_send()


def front(inner, taps, shift, wsel):
    return pl.pallas_call(
        front_kernel,
        out_shape=(
            jax.ShapeDtypeStruct((T + 16, C), F32),
            jax.ShapeDtypeStruct((T, C), F32),
            jax.ShapeDtypeStruct((TEN, ROWS, WIDE), BF16),
        ),
        in_specs=[VMEM] * 4,
        out_specs=(VMEM,) * 3,
        scratch_shapes=[
            pltpu.VMEM((16, C), BF16),
            pltpu.VMEM((128, C), BF16),
            pltpu.VMEM((TEN, ROWS, WIDE), BF16),
            pltpu.VMEM((TEN, ROWS, WIDE), BF16),
            pltpu.SemaphoreType.DMA,
            pltpu.SemaphoreType.DMA,
        ] + [pltpu.SemaphoreType.DMA((TEN,))] * 4,
        compiler_params=pltpu.CompilerParams(
            collective_id=0, has_side_effects=True, vmem_limit_bytes=32 << 20
        ),
        name="front",
    )(inner, taps, shift, wsel)


def spread(tile, first):
    rows = T * N
    repeat = (iota((rows, T), 0) // N == iota((rows, T), 1)).astype(BF16)
    each = dot_nn(repeat, tile)
    mine = iota((rows, 128), 1) % 64 == iota((rows, 128), 0) % N + first
    return dot_nn(jnp.where(mine, each, 0.0).astype(BF16), jnp.ones((128, 128), BF16))


def summary_kernel(
    pre, proj, wdelta, bias, dlog, gate, grad, raw, deltas, dx, ocot, bspread, cspread, ends
):
    flat = proj[...].reshape(T, WIDE)
    value = dot_nt(flat[:, :RANK], wdelta[...]) + bias[...]
    raw[...] = value
    step = jnp.maximum(value, 0.0) + jnp.log1p(jnp.exp(-jnp.abs(value)))
    deltas[...] = step
    v = pre[...]
    dx[...] = step * (v * sigmoid(v))
    g = gate[...].astype(F32)
    ocot[...] = grad[...].astype(F32) * (g * sigmoid(g))
    bspread[...] = spread(flat[:, RANK:], 0).reshape(T, N, 128)
    cspread[...] = spread(flat[:, RANK:], N).reshape(T, N, 128)

    def half(h, _):
        lanes = pl.ds(pl.multiple_of(h * H, H), H)
        rate = jnp.exp(dlog[:, lanes]) * (-LOG2E)

        def steps(block, carried):
            state, decay, flow = carried
            for i in range(8):
                t = block * 8 + i
                row = pl.ds(t, 1)
                d = jnp.exp2(deltas[row, lanes] * rate)
                b = jnp.concatenate([bspread[t]] * (H // 128), 1)
                c = jnp.concatenate([cspread[t]] * (H // 128), 1)
                state = d * state + dx[row, lanes] * b
                decay = decay * d
                flow = flow + decay * (ocot[row, lanes] * c)
            return state, decay, flow

        zero = jnp.zeros((N, H), F32)
        state, decay, flow = lax.fori_loop(0, T // 8, steps, (zero, zero + 1.0, zero))
        for r in range(N // 8):
            for k in range(H // 128):
                at = r * 8 + h * (H // 128) + k
                part = (slice(8 * r, 8 * r + 8), slice(128 * k, 128 * k + 128))
                ends[at, 0] = state[part]
                ends[at, 1] = decay[part]
                ends[at + 16, 0] = flow[part]
                ends[at + 16, 1] = decay[part]
        return 0

    lax.fori_loop(0, C // H, half, 0)


def summary(pre, proj, wdelta, bias, dlog, gate, grad):
    full = jax.ShapeDtypeStruct((T, C), F32)
    wide = jax.ShapeDtypeStruct((T, N, 128), F32)
    return pl.pallas_call(
        summary_kernel,
        out_shape=(full, full, full, full, wide, wide, jax.ShapeDtypeStruct((CTX, 2, 8, 128), F32)),
        in_specs=[VMEM] * 7,
        out_specs=(VMEM,) * 7,
        compiler_params=pltpu.CompilerParams(vmem_limit_bytes=48 << 20),
        name="summary",
    )(pre, proj, wdelta, bias, dlog, gate, grad)


def border_kernel(ends, borders, got, back, ss, sr, bs, br):
    me = lax.axis_index("context")
    greet("context", CTX)
    pl.semaphore_wait(pltpu.get_barrier_semaphore(), CTX - 1)
    out = Exchange(ends, got, ss, sr, "context", CTX)
    out.start()
    got[me] = ends[me]
    out.wait_recv()
    backward = me // 16

    def follow(i, carried):
        at = i + backward * (CTX - 1 - 2 * i)
        back[at] = carried
        return got[at, 1] * carried + got[at, 0]

    lax.fori_loop(0, CTX, follow, jnp.zeros((8, 128), F32))
    home = Exchange(back, borders, bs, br, "context", CTX)
    home.start()
    borders[me] = back[me]
    home.wait_recv()
    out.wait_send()
    home.wait_send()


def border(ends):
    return pl.pallas_call(
        border_kernel,
        out_shape=jax.ShapeDtypeStruct((CTX, 8, 128), F32),
        in_specs=[VMEM],
        out_specs=VMEM,
        scratch_shapes=[
            pltpu.VMEM((CTX, 2, 8, 128), F32),
            pltpu.VMEM((CTX, 8, 128), F32),
        ] + [pltpu.SemaphoreType.DMA((CTX,))] * 4,
        compiler_params=pltpu.CompilerParams(collective_id=1, has_side_effects=True),
        name="border",
    )(ends)


def gradient_kernel(
    pre, proj, wdelta, dlog, skip, gate, grad, raw, deltas, dx, ocot, bspread, cspread, borders,
    gate_grad, direct, psel, dterm, prm,
    before, bblock, cblock, y, along, wsum, isum, osum, work, rates,
):
    flat = proj[...].reshape(T, WIDE)
    column = iota((128, 16 * N), 1)
    same = iota((T, 16 * N), 0) % 16 == column // N
    lane = iota((128, 16 * N), 0) % 64
    bblock[...] = jnp.where(
        same, dot_nn(flat[:, RANK:], (lane == column % N).astype(BF16)), 0.0
    ).astype(BF16)
    cblock[...] = jnp.where(
        same, dot_nn(flat[:, RANK:], (lane == column % N + N).astype(BF16)), 0.0
    ).astype(BF16)
    ones = (iota((16, 16 * N), 0) == iota((16, 16 * N), 1) // N).astype(BF16)
    wide = H // 128

    def edges(first, h):
        return jnp.concatenate(
            [
                jnp.concatenate([borders[first + r * 8 + h * wide + k] for k in range(wide)], 1)
                for r in range(N // 8)
            ],
            0,
        )

    def lane_sum(v):
        return functools.reduce(jnp.add, [v[:, 128 * k : 128 * k + 128] for k in range(wide)])

    def half(h, _):
        lanes = pl.ds(pl.multiple_of(h * H, H), H)
        rate = -jnp.exp(dlog[:, lanes])
        rate2 = rate * LOG2E

        def forward(block, state):
            for i in range(16):
                t = block * 16 + i
                row = pl.ds(t, 1)
                before[t] = state
                d = jnp.exp2(deltas[row, lanes] * rate2)
                b = jnp.concatenate([bspread[t]] * wide, 1)
                state = d * state + dx[row, lanes] * b
                work[N * i : N * i + N, :] = state.astype(BF16)
                osum[h, t] = lane_sum(state * ocot[row, lanes])
            rows = pl.ds(pl.multiple_of(block * 16, 16), 16)
            y[rows, lanes] = dot_nn(cblock[rows, :], work[...])
            return state

        lax.fori_loop(0, T // 16, forward, edges(0, h))

        def backward(index, carried):
            flow, total = carried
            block = T // 16 - 1 - index
            for i in reversed(range(16)):
                t = block * 16 + i
                row = pl.ds(t, 1)
                delta = deltas[row, lanes]
                c = jnp.concatenate([cspread[t]] * wide, 1)
                adjoint = ocot[row, lanes] * c + flow
                isum[h, t] = lane_sum(adjoint * dx[row, lanes])
                work[N * i : N * i + N, :] = adjoint.astype(BF16)
                flow = jnp.exp2(delta * rate2) * adjoint
                weighted = flow * before[t]
                total = total + weighted * delta
                rates[N * i : N * i + N, :] = (weighted * rate).astype(BF16)
            rows = pl.ds(pl.multiple_of(block * 16, 16), 16)
            along[rows, lanes] = dot_nn(bblock[rows, :], work[...])
            wsum[rows, lanes] = dot_nn(ones, rates[...])
            return flow, total

        _, total = lax.fori_loop(0, T // 16, backward, (edges(16, h), jnp.zeros((N, H), F32)))
        prm[0:N, lanes] = total * rate
        return 0

    lax.fori_loop(0, C // H, half, 0)

    v = pre[...]
    conv = v * sigmoid(v)
    cot = ocot[...]
    gain = skip[...]
    g = gate[...].astype(F32)
    outputs = y[...] + gain * conv
    gate_grad[...] = (grad[...].astype(F32) * outputs * silu_slope(g)).astype(BF16)
    near = along[...]
    direct[...] = gain * cot + deltas[...] * near
    raw_cot = (wsum[...] + conv * near) * sigmoid(raw[...])
    raw_half = raw_cot.astype(BF16)
    prm[N : N + 1, :] = jnp.sum(raw_cot, axis=0, keepdims=True)
    prm[N + 1 : N + 2, :] = jnp.sum(cot * conv, axis=0, keepdims=True)
    prm[N + 2 :, :] = jnp.zeros((6, C), F32)
    psel[:, :, :RANK] = dot_nn(raw_half, wdelta[...]).astype(BF16).reshape(TEN, ROWS, RANK)
    dterm[...] = dot_tn(flat[:, :RANK], raw_half).astype(BF16).reshape(CTX, RANK // CTX, C)

    unit = jnp.ones((128, 128), BF16)
    spot = iota((16 * N, 128), 1)
    which = iota((16 * N, 128), 0) % N

    def gather(block, _):
        rows = pl.ds(pl.multiple_of(block * 16, 16), 16)
        inputs = (isum[0, rows] + isum[1, rows]).reshape(16 * N, 128).astype(BF16)
        outs = (osum[0, rows] + osum[1, rows]).reshape(16 * N, 128).astype(BF16)
        both = jnp.where(spot == which, dot_nn(inputs, unit), 0.0) + jnp.where(
            spot == which + N, dot_nn(outs, unit), 0.0
        )
        psel[block, :, RANK:] = dot_nn(ones, both.astype(BF16)).astype(BF16)
        return 0

    lax.fori_loop(0, T // 16, gather, 0)


def gradient(*args):
    full = jax.ShapeDtypeStruct((T, C), F32)
    return pl.pallas_call(
        gradient_kernel,
        out_shape=(
            jax.ShapeDtypeStruct((T, C), BF16),
            full,
            jax.ShapeDtypeStruct((TEN, ROWS, WIDE), BF16),
            jax.ShapeDtypeStruct((CTX, RANK // CTX, C), BF16),
            jax.ShapeDtypeStruct((24, C), F32),
        ),
        in_specs=[VMEM] * 14,
        out_specs=(VMEM,) * 5,
        scratch_shapes=[
            pltpu.VMEM((T, N, H), F32),
            pltpu.VMEM((T, 16 * N), BF16),
            pltpu.VMEM((T, 16 * N), BF16),
            pltpu.VMEM((T, C), F32),
            pltpu.VMEM((T, C), F32),
            pltpu.VMEM((T, C), F32),
            pltpu.VMEM((2, T, N, 128), F32),
            pltpu.VMEM((2, T, N, 128), F32),
            pltpu.VMEM((16 * N, H), BF16),
            pltpu.VMEM((16 * N, H), BF16),
        ],
        compiler_params=pltpu.CompilerParams(vmem_limit_bytes=56 << 20),
        name="gradient",
    )(*args)


def back_kernel(
    psel, dterm, prm, pre, pad, direct, wsel, taps,
    inner_grad, sel_main, sel_extra, delta, params,
    got_sel, sel, got_d, main, got_m, extra, got_x, own, got_p, trail, edge, late,
    es, er, ts, tr, gs, gr, ds, dr, ms, mr, xs, xr, ps, pr, qs, qr,
):
    ctx, ten = lax.axis_index("context"), lax.axis_index("tensor")
    greet("tensor", TEN)
    greet("context", CTX)
    pl.semaphore_wait(pltpu.get_barrier_semaphore(), TEN - 1 + CTX - 1)

    scatter = Exchange(psel, got_sel, ts, tr, "tensor", TEN)
    scatter.start()
    deltas = Exchange(dterm, got_d, ds, dr, "context", CTX)
    deltas.start()
    got_sel[ten] = psel[ten]
    got_d[ctx] = dterm[ctx]
    value = pre[...]
    half = (value * sigmoid(value)).astype(BF16)
    target = iota((WIDE, WIDE), 0)
    source = iota((WIDE, WIDE), 1)
    order = jnp.where(target < RANK, target // 16 * 17 + target % 16, (target - RANK) * 17 + 16)
    order = ((order == source) & (target < PROJ)).astype(BF16)

    scatter.wait_recv()
    sel[ten] = jnp.sum(got_sel[...].astype(F32), axis=0).astype(BF16)
    gather = Exchange(sel, sel, gs, gr, "tensor", TEN, same=True)
    gather.start()
    gather.wait_recv()
    select_cot = sel[...].reshape(T, WIDE)

    turned = dot_nt(order, select_cot).astype(BF16)
    main[...] = dot_nn(turned[:RANK, :], half).astype(BF16).reshape(CTX, 16, C)
    mains = Exchange(main, got_m, ms, mr, "context", CTX)
    mains.start()
    got_m[ctx] = main[ctx]
    extra[...] = dot_nn(turned[RANK : RANK + CTX, :], half).reshape(CTX, 1, C)
    extras = Exchange(extra, got_x, xs, xr, "context", CTX)
    extras.start()
    got_x[ctx] = extra[ctx]

    cot = direct[...] + dot_nn(select_cot[:, :PROJ], wsel[...])
    cot = cot * silu_slope(value)
    trail[0:T, :] = cot
    edge[...] = cot[0:8, :]
    below = to_neighbour(edge, late, es, er, -1)
    below.start()
    rows = [prm[N : N + 2, :], jnp.sum(cot, axis=0, keepdims=True)]
    for k in range(TAPS):
        rows.append(
            jnp.sum(cot * pad[pl.ds(16 - TAPS + 1 + k, T), :], axis=0, keepdims=True)
        )
    rows.append(jnp.zeros((1, C), F32))
    rows = jnp.concatenate(rows, 0)
    for k in range(C // 128):
        lanes = slice(128 * k, 128 * k + 128)
        own[k] = prm[0:8, lanes]
        own[8 + k] = prm[8:16, lanes]
        own[16 + k] = rows[:, lanes]
        own[24 + k] = jnp.zeros((8, 128), F32)
    sums = Exchange(own, got_p, ps, pr, "context", CTX)
    sums.start()
    got_p[ctx] = own[ctx]

    below.wait()
    trail[T:, :] = late[...] * (ctx < CTX - 1).astype(F32)
    result = jnp.zeros((T, C), F32)
    for k in range(TAPS):
        result = result + taps[k : k + 1, :] * trail[pl.ds(TAPS - 1 - k, T), :]
    inner_grad[...] = result.astype(BF16)

    sums.wait_recv()
    params[ctx] = jnp.sum(got_p[...], axis=0)
    spreads = Exchange(params, params, qs, qr, "context", CTX, same=True)
    spreads.start()

    def add_up(ref, shape):
        return lax.fori_loop(
            0, CTX, lambda i, total: total + ref[i].astype(F32), jnp.zeros(shape, F32)
        )

    deltas.wait_recv()
    delta[...] = add_up(got_d, (16, C))
    extras.wait_recv()
    sel_extra[...] = add_up(got_x, (1, C))
    mains.wait_recv()
    sel_main[...] = add_up(got_m, (16, C))
    spreads.wait_recv()
    for exchange in (scatter, deltas, gather, mains, extras, sums, spreads):
        exchange.wait_send()


def back(*args):
    def pair(*shape):
        return [pltpu.VMEM(shape, BF16)]

    return pl.pallas_call(
        back_kernel,
        out_shape=(
            jax.ShapeDtypeStruct((T, C), BF16),
            jax.ShapeDtypeStruct((16, C), F32),
            jax.ShapeDtypeStruct((1, C), F32),
            jax.ShapeDtypeStruct((16, C), F32),
            jax.ShapeDtypeStruct((CTX, 8, 128), F32),
        ),
        in_specs=[VMEM] * 8,
        out_specs=(VMEM,) * 5,
        scratch_shapes=[
            pltpu.VMEM((TEN, ROWS, WIDE), BF16),
            pltpu.VMEM((TEN, ROWS, WIDE), BF16),
            pltpu.VMEM((CTX, 16, C), BF16),
            pltpu.VMEM((CTX, 16, C), BF16),
            pltpu.VMEM((CTX, 16, C), BF16),
            pltpu.VMEM((CTX, 1, C), F32),
            pltpu.VMEM((CTX, 1, C), F32),
            pltpu.VMEM((CTX, 8, 128), F32),
            pltpu.VMEM((CTX, 8, 128), F32),
            pltpu.VMEM((T + 8, C), F32),
            pltpu.VMEM((8, C), F32),
            pltpu.VMEM((8, C), F32),
            pltpu.SemaphoreType.DMA,
            pltpu.SemaphoreType.DMA,
        ]
        + [pltpu.SemaphoreType.DMA((TEN,))] * 4
        + [pltpu.SemaphoreType.DMA((CTX,))] * 10,
        compiler_params=pltpu.CompilerParams(
            collective_id=2, has_side_effects=True, vmem_limit_bytes=48 << 20
        ),
        name="back",
    )(*args)


def body(
    inner_in, gate_in, out_grad, kernel, kernel_shift, select_proj, delta_proj, delta_bias,
    decay_log, skip_gain,
):
    taps = kernel.T
    dlog = decay_log.T
    pad, pre, proj = front(inner_in, taps, kernel_shift[None], select_proj)
    raw, deltas, dx, ocot, bspread, cspread, ends = summary(
        pre, proj, delta_proj, delta_bias[None], dlog, gate_in, out_grad
    )
    borders = border(ends)
    gate_grad, direct, psel, dterm, prm = gradient(
        pre, proj, delta_proj, dlog, skip_gain[None], gate_in, out_grad,
        raw, deltas, dx, ocot, bspread, cspread, borders,
    )
    inner_grad, sel_main, sel_extra, delta, params = back(
        psel, dterm, prm, pre, pad, direct, select_proj, taps
    )
    rows = params.reshape(4, 8, 8, 128).transpose(0, 2, 1, 3).reshape(32, C)
    return (
        inner_grad,
        gate_grad,
        rows[19:23].T,
        rows[18],
        jnp.concatenate([sel_main, sel_extra], 0),
        delta.T,
        rows[16],
        rows[0:16].T,
        rows[17],
    )


def solution(mesh):
    return jax.shard_map(
        body,
        mesh=mesh,
        in_specs=(
            P("context", "tensor"),
            P("context", "tensor"),
            P("context", "tensor"),
            P("tensor", None),
            P("tensor"),
            P(None, "tensor"),
            P("tensor", None),
            P("tensor"),
            P("tensor", None),
            P("tensor"),
        ),
        out_specs=(
            P("context", "tensor"),
            P("context", "tensor"),
            P("tensor", None),
            P("tensor"),
            P("context", "tensor"),
            P("tensor", "context"),
            P("tensor"),
            P("tensor", None),
            P("tensor"),
        ),
        check_vma=False,
    )
```

time: 1430 us -> 139 us (0.10); the launches traced: 1400 us -> 139 us
  local copies, waits for them, and re-layouts: 455 us -> 16.8 us
  other arithmetic: 258 us -> 0.65 us
  waiting for transfers between devices: 228 us -> 0 us
  blocking collectives: 221 us -> 0 us
  starting transfers between devices: 185 us -> 0 us
  Pallas kernels: 0 us -> 121 us
  matrix products: 37.2 us -> 0 us
    pad x64 -> x0, local copies, waits for them, and re-layouts: 319 us -> none  [scan_pairs(): lax.associative_scan(combine, (decays, additions), axis=0, reverse=backward)]
    add x127 -> x0, other arithmetic: 181 us -> none  [the longest x40 85.6 us: scan_pairs(): lax.associative_scan(combine, (decays, additions), axis=0, reverse=backward)]
    ppermute x64 -> x0, waiting for transfers between devices: 158 us -> none  [passed_along(): lax.ppermute(value, axis, [(source, source + steps) for source in range(l...]
    ppermute x64 -> x0, starting transfers between devices: 147 us -> none  [passed_along(): lax.ppermute(value, axis, [(source, source + steps) for source in range(l...]
    psum x2 -> x0, blocking collectives: 145 us -> none  [the longest x1 119 us: body(): lax.psum((kernel_part, shift_part, bias_part, decay_part, skip_part), 'co...]
    pallas_call x0 -> x5, Pallas kernels: none -> 121 us  [the longest x1 51.4 us: back(): pl.pallas_call(back_kernel, out_shape=(jax.ShapeDtypeStruct((T, C), BF16)...]
    unnamed x1 -> x0, blocking collectives: 76 us -> none
    psum x2 -> x0, waiting for transfers between devices: 69.5 us -> none  [the longest x1 69.5 us: body(): projected = lax.psum(partial_proj, 'tensor')]
  transfers between devices with their start and end apart: 77 -> 0, of which waited for: 33 -> 0; matrix products, arithmetic and copies ran while one was open for 6% -> 0% of each run, Pallas kernels for 0% -> 0%
where the time goes in v1:
time: 139 us
  Pallas kernels  121 us (87%)
  local copies, waits for them, and re-layouts  16.8 us (12%)
    pallas_call x1, Pallas kernels, back(): pl.pallas_call(back_kernel, out_shape=(jax.ShapeDtypeStruct((T, C), BF16)...  51.4 us
    pallas_call x1, Pallas kernels, border(): pl.pallas_call(border_kernel, out_shape=jax.ShapeDtypeStruct((CTX, 8, 128...  24.2 us
    pallas_call x1, Pallas kernels, front(): pl.pallas_call(front_kernel, out_shape=(jax.ShapeDtypeStruct((T + 16, C),...  21.3 us
    pallas_call x1, Pallas kernels, gradient(): pl.pallas_call(gradient_kernel, out_shape=(jax.ShapeDtypeStruct((T, C), B...  17.8 us
    unnamed x50, local copies, waits for them, and re-layouts  14.9 us
    pallas_call x1, Pallas kernels, summary(): pl.pallas_call(summary_kernel, out_shape=(full, full, full, full, wide, w...  5.89 us

profile of v1, /device:TPU:1, one launch (start us, length us, event | category | flops | bytes accessed | tf_op | source)
XLA Modules:
  0.0 138.8 jit_solution(13946842526472615806)
XLA Ops:
  0.6 0.0 copy-start.23
  0.7 0.0 copy-start.2
  0.7 1.2 copy-done.2
  1.9 0.0 copy-start.17
  1.9 0.9 copy-done.17
  2.9 0.0 copy-start.20
  2.9 0.7 copy-done.20
  3.6 0.0 copy-start.22
  3.6 0.7 copy-done.22
  4.3 0.0 copy-start.4
  4.3 21.3 %front.1 = (f32[144,1024]{1,0:T(8,128)S(1)}, f32[128,1024]{1,0:T(8,128)S(1)}, bf16[8,16,640]{2,1,0:T(8,128)(2,1)S(1)}) custom-call(bf16[128,1024]{1,0:T(8,128)(2,1)S(1)} %copy-done.17, f32[4,1024]{1,0:T(4,128)S(1)} %bitcast.25, f32[1,1024]{1,0:T(1,128)S(1)} %bitcast.28, bf16[544,1024]{1,0:T(8,128)(2,1)S(1)} %copy-done.2), custom_call_target="tpu_custom_call" | custom-call | tf_op jit(solution)/shard_map/front/pallas_call | solution.py:155
  25.6 0.0 copy-start
  25.6 0.0 copy-start.9
  25.6 0.0 copy-done.23
  25.6 0.0 copy-done.4
  25.6 0.0 copy-done.5
  25.7 0.0 copy-done.15
  25.7 5.9 %summary.1 = (f32[128,1024]{1,0:T(8,128)S(1)}, f32[128,1024]{1,0:T(8,128)S(1)}, f32[128,1024]{1,0:T(8,128)S(1)}, f32[128,1024]{1,0:T(8,128)S(1)}, f32[128,16,128...) custom-call(f32[128,1024]{1,0:T(8,128)S(1)} %get-tuple-element.29.pre, ...), custom_call_target="tpu_custom_call" | custom-call | tf_op jit(solution)/shard_map/summary/pallas_call | solution.py:237
  31.6 0.0 copy-done
  31.6 0.0 copy-done.9
  31.6 0.0 copy-start.7
  31.6 0.9 copy-done.7
  32.5 1.0 copy-done.8
  33.5 0.8 copy-done.10
  34.4 0.8 copy-done.11
  35.2 0.8 copy-done.12
  36.0 0.8 copy-done.13
  36.8 0.7 copy-done.16
  37.5 24.2 %border.1.borders = f32[32,8,128]{2,1,0:T(8,128)} custom-call(f32[32,2,8,128]{3,2,1,0:T(8,128)} %copy-done.16), custom_call_target="tpu_custom_call" | custom-call | tf_op jit(solution)/shard_map/border/pallas_call | solution.py:272
  61.7 0.0 copy-start.1
  61.7 0.0 copy-start.3
  61.7 0.0 copy-start.21
  61.7 17.8 %gradient.1 = (bf16[128,1024]{1,0:T(8,128)(2,1)}, f32[128,1024]{1,0:T(8,128)}, bf16[8,16,640]{2,1,0:T(8,128)(2,1)}, bf16[32,16,1024]{2,1,0:T(8,128)(2,1)}, f32[24,1024]{1,0:T(8,128)}) custom-call(f32[128,1024]{1,0:T(8,128)} %copy-done, bf16[8,16,640]{2,1,0:T(8,128)(2,1)} %copy-done.9, bf16[1024,512]{1,0:T(8,128)(2,1)} %wdelta.3, f32[16,1024]{1,0:T(8,128)} %bitcast.20, ...), custom_call_target="tpu_custom_call" | custom-call | tf_op jit(solution)/shard_map/gradient/pallas_call | solution.py:399
  79.5 0.0 copy-done.1
  79.5 0.0 copy-done.3
  79.5 0.0 copy-done.21
  79.5 0.0 copy-start.6
  79.5 1.2 copy-done.6
  80.7 1.0 copy-done.14
  81.8 0.9 copy-done.18
  82.7 0.9 copy-done.19
  83.6 51.4 %back.1 = (bf16[128,1024]{1,0:T(8,128)(2,1)S(1)}, f32[16,1024]{1,0:T(8,128)S(1)}, f32[1,1024]{1,0:T(1,128)S(1)}, f32[16,1024]{1,0:T(8,128)S(1)}, f32[32,8,128]{2,1,0:T(8,128)S(1)}) custom-call(bf16[8,16,640]{2,1,0:T(8,128)(2,1)S(1)} %copy-done.18, bf16[32,16,1024]{2,1,0:T(8,128)(2,1)S(1)} %copy-done.6, f32[24,1024]{1,0:T(8,128)S(1)} %copy-done.19, ...), custom_call_target="tpu_custom_call" | custom-call | tf_op jit(solution)/shard_map/back/pallas_call | solution.py:523
  135.0 0.6 fusion
  135.6 0.6 slice_bitcast_fusion.1
  136.2 0.6 slice_bitcast_fusion
  136.8 0.6 pad_maximum_fusion
  137.5 0.7 copy.21
  138.2 0.6 copy.22
  (11 shorter events, 0.0 us)
Async XLA Ops:
  0.6 25.0 %copy-start.23 = (f32[1024]{0:T(1024)S(1)}, f32[1024]{0:T(1024)}, u32[]{:S(2)}) copy-start(f32[1024]{0:T(1024)} %param.17) | copy-start | bytes 12292
  0.7 1.3 copy-start.2
  1.9 0.9 copy-start.17
  2.9 0.7 copy-start.20
  3.6 0.7 copy-start.22
  4.3 21.4 %copy-start.4 = (bf16[128,1024]{1,0:T(8,128)(2,1)S(1)}, bf16[128,1024]{1,0:T(8,128)(2,1)}, u32[]{:S(2)}) copy-start(bf16[128,1024]{1,0:T(8,128)(2,1)} %gate.3) | copy-start | bytes 786436
  4.3 21.4 %copy-start.5 = (bf16[128,1024]{1,0:T(8,128)(2,1)S(1)}, bf16[128,1024]{1,0:T(8,128)(2,1)}, u32[]{:S(2)}) copy-start(bf16[128,1024]{1,0:T(8,128)(2,1)} %grad.3) | copy-start | bytes 786436
  4.3 21.4 %copy-start.15 = (f32[1024,16]{0,1:T(8,128)S(1)}, f32[1024,16]{0,1:T(8,128)}, u32[]{:S(2)}) copy-start(f32[1024,16]{0,1:T(8,128)} %param.18) | copy-start | bytes 196612
  25.6 6.0 %copy-start = (f32[128,1024]{1,0:T(8,128)}, f32[128,1024]{1,0:T(8,128)S(1)}, u32[]{:S(2)}) copy-start(f32[128,1024]{1,0:T(8,128)S(1)} %get-tuple-element.29.pre) | copy-start | bytes 1572868
  25.6 6.0 %copy-start.9 = (bf16[8,16,640]{2,1,0:T(8,128)(2,1)}, bf16[8,16,640]{2,1,0:T(8,128)(2,1)S(1)}, u32[]{:S(2)}) copy-start(bf16[8,16,640]{2,1,0:T(8,128)(2,1)S(1)} %get-tuple-element.30.proj) | copy-start | bytes 491524
  31.6 1.0 copy-start.7
  32.5 1.0 copy-start.8
  33.5 0.8 copy-start.10
  34.4 0.8 copy-start.11
  35.1 0.8 copy-start.12
  36.0 0.8 copy-start.13
  36.8 0.7 copy-start.16
  61.7 17.8 %copy-start.1 = (f32[128,1024]{1,0:T(8,128)S(1)}, f32[128,1024]{1,0:T(8,128)}, u32[]{:S(2)}) copy-start(f32[128,1024]{1,0:T(8,128)} %copy-done) | copy-start | bytes 1572868
  61.7 17.8 %copy-start.3 = (bf16[544,1024]{1,0:T(8,128)(2,1)S(1)}, bf16[544,1024]{1,0:T(8,128)(2,1)}, u32[]{:S(2)}) copy-start(bf16[544,1024]{1,0:T(8,128)(2,1)} %wsel.3) | copy-start | bytes 3342340
  61.7 17.8 %copy-start.21 = (f32[1024,4]{0,1:T(4,128)S(1)}, f32[1024,4]{0,1:T(4,128)}, u32[]{:S(2)}) copy-start(f32[1024,4]{0,1:T(4,128)} %param.13) | copy-start | bytes 49156
  79.5 1.2 copy-start.6
  80.7 1.0 copy-start.14
  81.8 0.9 copy-start.18
  82.7 0.9 copy-start.19

commit v2 on v0

v2 whole, which is shorter than its diff:
```python
import functools

import jax
import jax.numpy as jnp
from jax import lax
from jax.experimental import pallas as pl
from jax.experimental.pallas import tpu as pltpu
from jax.sharding import PartitionSpec as P

N = 16
RANK = 512
TAPS = 4
PROJ = 544
WIDE = 640
T = 128
C = 1024
H = 512
CTX = 32
TEN = 8
ROWS = T // TEN
LOG2E = 1.4426950408889634
MESH = pl.DeviceIdType.MESH
F32 = jnp.float32
BF16 = jnp.bfloat16
VMEM = pl.BlockSpec(memory_space=pltpu.VMEM)


def dot_nn(a, b):
    return lax.dot_general(a, b, (((1,), (0,)), ((), ())), preferred_element_type=F32)


def dot_nt(a, b):
    return lax.dot_general(a, b, (((1,), (1,)), ((), ())), preferred_element_type=F32)


def dot_tn(a, b):
    return lax.dot_general(a, b, (((0,), (0,)), ((), ())), preferred_element_type=F32)


def iota(shape, axis):
    return lax.broadcasted_iota(jnp.int32, shape, axis)


def sigmoid(v):
    return jax.nn.sigmoid(v)


def silu_slope(v):
    s = sigmoid(v)
    return s * (1.0 + v * (1.0 - s))


def split_tile(v):
    high = v.astype(BF16).astype(F32)
    return jnp.where(iota(v.shape, 1) < 64, high, v - high).astype(BF16)


class Exchange:
    def __init__(self, src, dst, sems, axis, size, same=False, chips=False):
        self.src, self.dst, self.send, self.recv = src, dst, sems[0], sems[1]
        self.axis, self.size, self.same, self.chips = axis, size, same, chips

    def copy(self, off):
        me = lax.axis_index(self.axis)
        at = me // 2 if self.chips else me
        peer = lax.rem(at + off, self.size)
        return pltpu.make_async_remote_copy(
            src_ref=self.src.at[at] if self.same else self.src.at[peer],
            dst_ref=self.dst.at[at],
            send_sem=self.send.at[off],
            recv_sem=self.recv.at[off],
            device_id={self.axis: peer * 2 + lax.rem(me, 2) if self.chips else peer},
            device_id_type=MESH,
        )

    def start(self):
        lax.fori_loop(1, self.size, lambda off, _: (self.copy(off).start(), 0)[1], 0)

    def wait_recv(self):
        lax.fori_loop(1, self.size, lambda off, _: (self.copy(off).wait_recv(), 0)[1], 0)

    def wait_send(self):
        lax.fori_loop(1, self.size, lambda off, _: (self.copy(off).wait_send(), 0)[1], 0)


def greet(axis, size):
    me = lax.axis_index(axis)
    barrier = pltpu.get_barrier_semaphore()

    def signal(off, _):
        pl.semaphore_signal(
            barrier, inc=1, device_id={axis: lax.rem(me + off, size)}, device_id_type=MESH
        )
        return 0

    lax.fori_loop(1, size, signal, 0)


def to_neighbour(src, dst, send, recv, step):
    peer = lax.rem(lax.axis_index("context") + step + CTX, CTX)
    return pltpu.make_async_remote_copy(
        src_ref=src, dst_ref=dst, send_sem=send, recv_sem=recv,
        device_id={"context": peer}, device_id_type=MESH,
    )


def spread(tile, first):
    rows = T * N
    repeat = (iota((rows, T), 0) // N == iota((rows, T), 1)).astype(BF16)
    each = dot_nn(repeat, tile)
    mine = iota((rows, 128), 1) % 64 == iota((rows, 128), 0) % N + first
    return dot_nn(jnp.where(mine, each, 0.0).astype(BF16), jnp.ones((128, 128), BF16))


CHIPS = CTX // 2
HALVES = C // H
LT = H // 128

SCRATCH = (
    ("pad", (T + 16, C), F32),
    ("pre", (T, C), F32),
    ("conv", (T, C), F32),
    ("slope", (T, C), F32),
    ("half", (T, C), BF16),
    ("ocot", (T, C), F32),
    ("gslope", (T, C), F32),
    ("sig", (T, C), F32),
    ("deltas", (T, C), F32),
    ("dx", (T, C), F32),
    ("y", (T, C), F32),
    ("along", (T, C), F32),
    ("wsum", (T, C), F32),
    ("direct", (T, C), F32),
    ("halo", (16, C), BF16),
    ("wtail", (128, C), BF16),
    ("part", (TEN, ROWS, WIDE), BF16),
    ("got_part", (TEN, ROWS, WIDE), BF16),
    ("proj", (TEN, ROWS, WIDE), BF16),
    ("bspread", (T, N, 128), F32),
    ("cspread", (T, N, 128), F32),
    ("bblock", (T, 16 * N), BF16),
    ("cblock", (T, 16 * N), BF16),
    ("steps", (CTX, 8, 128), F32),
    ("ends", (CTX, 8, 128), F32),
    ("got_ends", (CTX, 8, 128), F32),
    ("decays", (CTX, 8, 128), F32),
    ("back", (CTX, 8, 128), F32),
    ("borders", (CTX, 8, 128), F32),
    ("before", (T, N, H), F32),
    ("isum", (HALVES, T, N, 128), F32),
    ("osum", (HALVES, T, N, 128), F32),
    ("work", (16 * N, H), BF16),
    ("rates", (16 * N, H), BF16),
    ("decay_part", (N, C), F32),
    ("psel", (TEN, ROWS, WIDE), BF16),
    ("got_psel", (TEN, ROWS, WIDE), BF16),
    ("sel", (TEN, ROWS, WIDE), BF16),
    ("order", (WIDE, WIDE), BF16),
    ("dterm", (2, CHIPS, 16, C), BF16),
    ("dpair", (CHIPS, 16, C), BF16),
    ("dsum", (CHIPS, 16, C), BF16),
    ("got_d", (CHIPS, 16, C), BF16),
    ("mterm", (2, CHIPS, 16, C), BF16),
    ("mpair", (CHIPS, 16, C), BF16),
    ("msum", (CHIPS, 16, C), BF16),
    ("got_m", (CHIPS, 16, C), BF16),
    ("own", (CTX, 2, 8, 128), F32),
    ("got_own", (CTX, 2, 8, 128), F32),
    ("trail", (T + 8, C), F32),
    ("edge", (8, C), F32),
    ("late", (8, C), F32),
)
INPUTS = (
    ("inner", (T, C), BF16),
    ("gate", (T, C), BF16),
    ("grad", (T, C), BF16),
    ("taps", (TAPS, C), F32),
    ("shift", (1, C), F32),
    ("wsel", (PROJ, C), BF16),
    ("wdelta", (C, RANK), BF16),
    ("bias", (1, C), F32),
    ("dlog", (N, C), F32),
    ("skip", (1, C), F32),
)
OUTPUTS = (
    ("inner_grad", (T, C), BF16),
    ("gate_grad", (T, C), BF16),
    ("sel_main", (16, C), F32),
    ("sel_extra", (8, 128), F32),
    ("delta_grad", (16, C), F32),
    ("params", (CTX, 8, 128), F32),
)
SEMS = (
    ("in", (len(INPUTS),)),
    ("halo", (2,)),
    ("part", (2, TEN)),
    ("proj", (2, TEN)),
    ("steps", (2, CTX)),
    ("ends", (2, CTX)),
    ("back", (2, CTX)),
    ("psel", (2, TEN)),
    ("sel", (2, TEN)),
    ("dpair", (2,)),
    ("dsum", (2, CHIPS)),
    ("mpair", (2,)),
    ("msum", (2, CHIPS)),
    ("own", (2, CTX)),
    ("params", (2, CTX)),
    ("edge", (2,)),
)


class Refs:
    pass


def tile_of(v, r, k):
    return v[8 * r : 8 * r + 8, 128 * k : 128 * k + 128]


def wide_of(v):
    return jnp.concatenate([v] * LT, 1)


def lane_sum(v):
    return functools.reduce(jnp.add, [v[:, 128 * k : 128 * k + 128] for k in range(LT)])


def half_lanes(h):
    return pl.ds(pl.multiple_of(h * H, H), H)


def rows_of(block):
    return pl.ds(pl.multiple_of(block * 16, 16), 16)


def convolve(z, first, rows):
    value = jnp.zeros((rows, C), F32) + z.shift[...]
    for k in range(TAPS):
        value = value + z.taps[k : k + 1, :] * z.pad[pl.ds(first + 16 - TAPS + 1 + k, rows), :]
    z.pre[pl.ds(first, rows), :] = value
    s = sigmoid(value)
    conv = value * s
    z.conv[pl.ds(first, rows), :] = conv
    z.half[pl.ds(first, rows), :] = conv.astype(BF16)
    z.slope[pl.ds(first, rows), :] = s * (1.0 + value * (1.0 - s))


def project(z, first, rows):
    half = z.half[pl.ds(first, rows), :]
    blocks = pl.ds(first // ROWS, rows // ROWS)
    shape = (rows // ROWS, ROWS)
    z.part[blocks, :, :RANK] = dot_nt(half, z.wsel[:RANK, :]).astype(BF16).reshape(*shape, RANK)
    z.part[blocks, :, RANK:] = split_tile(dot_nt(half, z.wtail[...])).reshape(*shape, 128)


def summarize(z):
    def half(h, _):
        lanes = half_lanes(h)
        rate = jnp.exp(z.dlog[:, lanes]) * (-LOG2E)

        def steps(block, carried):
            state, decay, flow = carried
            for i in range(8):
                t = block * 8 + i
                row = pl.ds(t, 1)
                d = jnp.exp2(z.deltas[row, lanes] * rate)
                state = d * state + z.dx[row, lanes] * wide_of(z.bspread[t])
                decay = decay * d
                flow = flow + decay * (z.ocot[row, lanes] * wide_of(z.cspread[t]))
            return state, decay, flow

        zero = jnp.zeros((N, H), F32)
        state, _, flow = lax.fori_loop(0, T // 8, steps, (zero, zero + 1.0, zero))
        for r in range(N // 8):
            for k in range(LT):
                at = r * 8 + h * LT + k
                z.ends[at] = tile_of(state, r, k)
                z.ends[at + 16] = tile_of(flow, r, k)
        return 0

    lax.fori_loop(0, HALVES, half, 0)


def recur(z):
    ones = (iota((16, 16 * N), 0) == iota((16, 16 * N), 1) // N).astype(BF16)

    def edges(first, h):
        return jnp.concatenate(
            [
                jnp.concatenate([z.borders[first + r * 8 + h * LT + k] for k in range(LT)], 1)
                for r in range(N // 8)
            ],
            0,
        )

    def half(h, _):
        lanes = half_lanes(h)
        rate = -jnp.exp(z.dlog[:, lanes])
        rate2 = rate * LOG2E

        def forward(block, state):
            for i in range(16):
                t = block * 16 + i
                row = pl.ds(t, 1)
                z.before[t] = state
                d = jnp.exp2(z.deltas[row, lanes] * rate2)
                state = d * state + z.dx[row, lanes] * wide_of(z.bspread[t])
                z.work[N * i : N * i + N, :] = state.astype(BF16)
                z.osum[h, t] = lane_sum(state * z.ocot[row, lanes])
            rows = rows_of(block)
            z.y[rows, lanes] = dot_nn(z.cblock[rows, :], z.work[...])
            return state

        lax.fori_loop(0, T // 16, forward, edges(0, h))

        def backward(index, carried):
            flow, total = carried
            block = T // 16 - 1 - index
            for i in reversed(range(16)):
                t = block * 16 + i
                row = pl.ds(t, 1)
                delta = z.deltas[row, lanes]
                adjoint = z.ocot[row, lanes] * wide_of(z.cspread[t]) + flow
                z.isum[h, t] = lane_sum(adjoint * z.dx[row, lanes])
                z.work[N * i : N * i + N, :] = adjoint.astype(BF16)
                flow = jnp.exp2(delta * rate2) * adjoint
                weighted = flow * z.before[t]
                total = total + weighted * delta
                z.rates[N * i : N * i + N, :] = (weighted * rate).astype(BF16)
            rows = rows_of(block)
            z.along[rows, lanes] = dot_nn(z.bblock[rows, :], z.work[...])
            z.wsum[rows, lanes] = dot_nn(ones, z.rates[...])
            return flow, total

        _, total = lax.fori_loop(0, T // 16, backward, (edges(16, h), jnp.zeros((N, H), F32)))
        z.decay_part[:, lanes] = total * rate
        return 0

    lax.fori_loop(0, HALVES, half, 0)

    unit = jnp.ones((128, 128), BF16)
    spot = iota((16 * N, 128), 1)
    which = iota((16 * N, 128), 0) % N

    def gather(block, _):
        rows = rows_of(block)
        inputs = functools.reduce(jnp.add, [z.isum[h, rows] for h in range(HALVES)])
        outs = functools.reduce(jnp.add, [z.osum[h, rows] for h in range(HALVES)])
        both = jnp.where(
            spot == which, dot_nn(inputs.reshape(16 * N, 128).astype(BF16), unit), 0.0
        ) + jnp.where(
            spot == which + N, dot_nn(outs.reshape(16 * N, 128).astype(BF16), unit), 0.0
        )
        z.psel[block, :, RANK:] = dot_nn(ones, both.astype(BF16)).astype(BF16)
        return 0

    lax.fori_loop(0, T // 16, gather, 0)


def to_sibling(src, dst, sems):
    me = lax.axis_index("context")
    return pltpu.make_async_remote_copy(
        src_ref=src, dst_ref=dst, send_sem=sems.at[0], recv_sem=sems.at[1],
        device_id={"context": me + 1 - 2 * lax.rem(me, 2)}, device_id_type=MESH,
    )


def layer_kernel(*refs):
    z, given, sem = Refs(), Refs(), Refs()
    refs = list(refs)
    for name, _, _ in INPUTS:
        setattr(given, name, refs.pop(0))
    for name, _, _ in OUTPUTS + INPUTS + SCRATCH:
        setattr(z, name, refs.pop(0))
    for name, _ in SEMS:
        setattr(sem, name, refs.pop(0))
    ctx, ten = lax.axis_index("context"), lax.axis_index("tensor")
    chip, core = ctx // 2, lax.rem(ctx, 2)

    loads = {}
    for i, (name, _, _) in enumerate(INPUTS):
        loads[name] = pltpu.make_async_copy(
            getattr(given, name), getattr(z, name), getattr(sem, "in").at[i]
        )

    for name in ("inner", "taps", "shift", "wsel", "gate", "grad", "dlog", "wdelta", "bias", "skip"):
        loads[name].start()
    greet("tensor", TEN)
    greet("context", CTX)

    for name in ("inner", "taps", "shift"):
        loads[name].wait()
    z.pad[16:, :] = z.inner[...].astype(F32)
    convolve(z, 16, T - 16)
    pl.semaphore_wait(pltpu.get_barrier_semaphore(), TEN - 1 + CTX - 1)
    halo = to_neighbour(z.inner.at[pl.ds(T - 16, 16)], z.halo, sem.halo.at[0], sem.halo.at[1], 1)
    halo.start()
    loads["wsel"].wait()
    tail = z.wsel[RANK:PROJ, :]
    z.wtail[0:32, :] = tail
    z.wtail[32:64, :] = jnp.zeros((32, C), BF16)
    z.wtail[64:96, :] = tail
    z.wtail[96:128, :] = jnp.zeros((32, C), BF16)
    project(z, 16, T - 16)
    halo.wait()
    z.pad[0:16, :] = z.halo[...].astype(F32) * (ctx > 0).astype(F32)
    convolve(z, 0, 16)
    project(z, 0, 16)
    scatter = Exchange(z.part, z.got_part, (sem.part.at[0], sem.part.at[1]), "tensor", TEN)
    scatter.start()
    z.got_part[ten] = z.part[ten]

    loads["gate"].wait()
    loads["grad"].wait()
    g = z.gate[...].astype(F32)
    s = sigmoid(g)
    grad = z.grad[...].astype(F32)
    z.ocot[...] = grad * (g * s)
    z.gslope[...] = grad * (s * (1.0 + g * (1.0 - s)))

    scatter.wait_recv()
    total = jnp.sum(z.got_part[...].astype(F32), axis=0)
    bc = total[:, RANK:]
    bc = bc + pltpu.roll(bc, 64, 1)
    z.proj[ten, :, :RANK] = total[:, :RANK].astype(BF16)
    z.proj[ten, :, RANK:] = split_tile(bc)
    gather = Exchange(
        z.proj, z.proj, (sem.proj.at[0], sem.proj.at[1]), "tensor", TEN, same=True
    )
    gather.start()
    target = iota((WIDE, WIDE), 0)
    source = iota((WIDE, WIDE), 1)
    place = target % 256
    order = jnp.where(
        target < RANK,
        (place // 16 * 2 + target // 256) * 17 + place % 16,
        (target - RANK) * 17 + 16,
    )
    z.order[...] = ((order == source) & (target < PROJ)).astype(BF16)
    for name in ("dlog", "wdelta", "bias", "skip"):
        loads[name].wait()
    gather.wait_recv()

    flat = z.proj[...].reshape(T, WIDE)
    raw = dot_nt(flat[:, :RANK], z.wdelta[...]) + z.bias[...]
    step = jnp.maximum(raw, 0.0) + jnp.log1p(jnp.exp(-jnp.abs(raw)))
    z.deltas[...] = step
    lengths = jnp.sum(step, axis=0, keepdims=True)
    for k in range(8):
        z.steps[ctx, k : k + 1, :] = lengths[:, 128 * k : 128 * k + 128]
    steps = Exchange(
        z.steps, z.steps, (sem.steps.at[0], sem.steps.at[1]), "context", CTX, same=True
    )
    steps.start()
    z.sig[...] = sigmoid(raw)
    z.dx[...] = step * z.conv[...]
    z.bspread[...] = spread(flat[:, RANK:], 0).reshape(T, N, 128)
    z.cspread[...] = spread(flat[:, RANK:], N).reshape(T, N, 128)
    summarize(z)

    ends = Exchange(z.ends, z.got_ends, (sem.ends.at[0], sem.ends.at[1]), "context", CTX)
    ends.start()
    z.got_ends[ctx] = z.ends[ctx]
    backward = ctx // 16
    at_row = pl.ds(pl.multiple_of(lax.rem(ctx, 16) // 8 * 8, 8), 8)
    at_lane = lax.rem(ctx, 8)
    rate = jnp.exp(z.dlog[at_row, pl.ds(pl.multiple_of(at_lane * 128, 128), 128)]) * (-LOG2E)
    steps.wait_recv()

    def shrink(i, _):
        z.decays[i] = jnp.exp2(rate * z.steps[i, pl.ds(at_lane, 1), :])
        return 0

    lax.fori_loop(0, CTX, shrink, 0)
    column = iota((128, 16 * N), 1)
    same = iota((T, 16 * N), 0) % 16 == column // N
    lane = iota((128, 16 * N), 0) % 64
    z.bblock[...] = jnp.where(
        same, dot_nn(flat[:, RANK:], (lane == column % N).astype(BF16)), 0.0
    ).astype(BF16)
    z.cblock[...] = jnp.where(
        same, dot_nn(flat[:, RANK:], (lane == column % N + N).astype(BF16)), 0.0
    ).astype(BF16)
    ends.wait_recv()

    def follow(i, carried):
        at = i + backward * (CTX - 1 - 2 * i)
        z.back[at] = carried
        return z.decays[at] * carried + z.got_ends[at]

    lax.fori_loop(0, CTX, follow, jnp.zeros((8, 128), F32))
    home = Exchange(z.back, z.borders, (sem.back.at[0], sem.back.at[1]), "context", CTX)
    home.start()
    z.borders[ctx] = z.back[ctx]
    home.wait_recv()

    recur(z)

    near = z.along[...]
    raw_cot = (z.wsum[...] + z.conv[...] * near) * z.sig[...]
    raw_half = raw_cot.astype(BF16)
    z.psel[:, :, :RANK] = dot_nn(raw_half, z.wdelta[...]).astype(BF16).reshape(TEN, ROWS, RANK)
    scatter2 = Exchange(z.psel, z.got_psel, (sem.psel.at[0], sem.psel.at[1]), "tensor", TEN)
    scatter2.start()
    z.got_psel[ten] = z.psel[ten]

    term = dot_tn(flat[:, :RANK], raw_half).astype(BF16).reshape(CHIPS, 2, 16, C)
    z.dterm[0] = term[:, 0]
    z.dterm[1] = term[:, 1]
    dpair = to_sibling(z.dterm.at[1 - core], z.dpair, sem.dpair)
    dpair.start()
    cot = z.ocot[...]
    gain = z.skip[...]
    z.gate_grad[...] = (z.gslope[...] * (z.y[...] + gain * z.conv[...])).astype(BF16)
    z.direct[...] = gain * cot + z.deltas[...] * near
    early = [
        jnp.sum(raw_cot, axis=0, keepdims=True),
        jnp.sum(cot * z.conv[...], axis=0, keepdims=True),
    ]
    dpair.wait()
    z.dsum[...] = (z.dterm[core].astype(F32) + z.dpair[...].astype(F32)).astype(BF16)
    deltas = Exchange(
        z.dsum, z.got_d, (sem.dsum.at[0], sem.dsum.at[1]), "context", CHIPS, chips=True
    )
    deltas.start()
    z.got_d[chip] = z.dsum[chip]

    scatter2.wait_recv()
    z.sel[ten] = jnp.sum(z.got_psel[...].astype(F32), axis=0).astype(BF16)
    gather2 = Exchange(z.sel, z.sel, (sem.sel.at[0], sem.sel.at[1]), "tensor", TEN, same=True)
    gather2.start()
    gather2.wait_recv()
    select_cot = z.sel[...].reshape(T, WIDE)

    turned = dot_nt(z.order[...], select_cot).astype(BF16)
    z.mterm[...] = dot_nn(turned[:RANK, :], z.half[...]).astype(BF16).reshape(2, CHIPS, 16, C)
    mpair = to_sibling(z.mterm.at[1 - core], z.mpair, sem.mpair)
    mpair.start()
    extra = dot_nn(turned[RANK : RANK + CTX, :], z.half[...])
    for k in range(8):
        z.own[:, 1, k, :] = extra[:, 128 * k : 128 * k + 128]
    pre_cot = (z.direct[...] + dot_nn(select_cot[:, :PROJ], z.wsel[...])) * z.slope[...]
    z.trail[0:T, :] = pre_cot
    z.edge[...] = pre_cot[0:8, :]
    below = to_neighbour(z.edge, z.late, sem.edge.at[0], sem.edge.at[1], -1)
    below.start()
    mpair.wait()
    z.msum[...] = (z.mterm[core].astype(F32) + z.mpair[...].astype(F32)).astype(BF16)
    mains = Exchange(
        z.msum, z.got_m, (sem.msum.at[0], sem.msum.at[1]), "context", CHIPS, chips=True
    )
    mains.start()
    z.got_m[chip] = z.msum[chip]

    late = [jnp.sum(pre_cot, axis=0, keepdims=True)]
    for k in range(TAPS):
        late.append(
            jnp.sum(pre_cot * z.pad[pl.ds(16 - TAPS + 1 + k, T), :], axis=0, keepdims=True)
        )
    rows = jnp.concatenate(early + late + [jnp.zeros((1, C), F32)], 0)
    for k in range(8):
        lanes = slice(128 * k, 128 * k + 128)
        z.own[k, 0] = z.decay_part[0:8, lanes]
        z.own[8 + k, 0] = z.decay_part[8:16, lanes]
        z.own[16 + k, 0] = rows[:, lanes]
        z.own[24 + k, 0] = jnp.zeros((8, 128), F32)
    sums = Exchange(z.own, z.got_own, (sem.own.at[0], sem.own.at[1]), "context", CTX)
    sums.start()
    z.got_own[ctx] = z.own[ctx]

    below.wait()
    z.trail[T:, :] = z.late[...] * (ctx < CTX - 1).astype(F32)
    result = jnp.zeros((T, C), F32)
    for k in range(TAPS):
        result = result + z.taps[k : k + 1, :] * z.trail[pl.ds(TAPS - 1 - k, T), :]
    z.inner_grad[...] = result.astype(BF16)
    deltas.wait_recv()
    z.delta_grad[...] = jnp.sum(z.got_d[...].astype(F32), axis=0)

    sums.wait_recv()
    z.params[ctx] = jnp.sum(z.got_own[:, 0], axis=0)
    spreads = Exchange(
        z.params, z.params, (sem.params.at[0], sem.params.at[1]), "context", CTX, same=True
    )
    spreads.start()
    z.sel_extra[...] = jnp.sum(z.got_own[:, 1], axis=0)
    mains.wait_recv()
    z.sel_main[...] = jnp.sum(z.got_m[...].astype(F32), axis=0)
    spreads.wait_recv()
    for exchange in (scatter, gather, steps, ends, home, scatter2, deltas, gather2, mains, sums, spreads):
        exchange.wait_send()


def layer(*args):
    return pl.pallas_call(
        layer_kernel,
        out_shape=[jax.ShapeDtypeStruct(shape, kind) for _, shape, kind in OUTPUTS],
        in_specs=[pl.BlockSpec(memory_space=pl.ANY)] * len(INPUTS),
        out_specs=[VMEM] * len(OUTPUTS),
        scratch_shapes=[pltpu.VMEM(shape, kind) for _, shape, kind in INPUTS + SCRATCH]
        + [pltpu.SemaphoreType.DMA(shape) for _, shape in SEMS],
        compiler_params=pltpu.CompilerParams(
            collective_id=0, has_side_effects=True, vmem_limit_bytes=56 << 20
        ),
        name="layer",
    )(*args)


def finish_kernel(
    inner_grad, gate_grad, sel_main, sel_extra, delta, params,
    inner_out, gate_out, taps_out, shift_out, sel_out, delta_out, bias_out, decay_out, skip_out,
):
    inner_out[...] = inner_grad[...]
    gate_out[...] = gate_grad[...]
    sel_out[0:16, :] = sel_main[...]
    delta_out[...] = delta[...]
    for k in range(8):
        lanes = slice(128 * k, 128 * k + 128)
        sel_out[16:17, lanes] = sel_extra[k : k + 1, :]
        decay_out[0:8, lanes] = params[k]
        decay_out[8:16, lanes] = params[8 + k]
        rows = params[16 + k]
        bias_out[:, lanes] = rows[0:1, :]
        skip_out[:, lanes] = rows[1:2, :]
        shift_out[:, lanes] = rows[2:3, :]
        taps_out[:, lanes] = rows[3:7, :]


def finish(*args):
    shapes = ((T, C), (T, C), (TAPS, C), (1, C), (17, C), (16, C), (1, C), (N, C), (1, C))
    return pl.pallas_call(
        finish_kernel,
        out_shape=[
            jax.ShapeDtypeStruct(shape, BF16 if i < 2 else F32) for i, shape in enumerate(shapes)
        ],
        in_specs=[VMEM] * 6,
        out_specs=[VMEM] * 9,
        name="finish",
    )(*args)


def body(
    inner_in, gate_in, out_grad, kernel, kernel_shift, select_proj, delta_proj, delta_bias,
    decay_log, skip_gain,
):
    parts = layer(
        inner_in, gate_in, out_grad, kernel.T, kernel_shift[None], select_proj, delta_proj,
        delta_bias[None], decay_log.T, skip_gain[None],
    )
    inner_grad, gate_grad, taps, shift, select, delta, bias, decay, skip = finish(*parts)
    return (
        inner_grad, gate_grad, taps.T, shift[0], select, delta.T, bias[0], decay.T, skip[0],
    )


def solution(mesh):
    return jax.shard_map(
        body,
        mesh=mesh,
        in_specs=(
            P("context", "tensor"),
            P("context", "tensor"),
            P("context", "tensor"),
            P("tensor", None),
            P("tensor"),
            P(None, "tensor"),
            P("tensor", None),
            P("tensor"),
            P("tensor", None),
            P("tensor"),
        ),
        out_specs=(
            P("context", "tensor"),
            P("context", "tensor"),
            P("tensor", None),
            P("tensor"),
            P("context", "tensor"),
            P("tensor", "context"),
            P("tensor"),
            P("tensor", None),
            P("tensor"),
        ),
        check_vma=False,
    )
```

time: 1430 us -> 97.4 us (0.07); the launches traced: 1400 us -> 97.2 us
  local copies, waits for them, and re-layouts: 455 us -> 0 us
  other arithmetic: 258 us -> 0 us
  waiting for transfers between devices: 228 us -> 0 us
  blocking collectives: 221 us -> 0 us
  starting transfers between devices: 185 us -> 0 us
  Pallas kernels: 0 us -> 96.6 us
  matrix products: 37.2 us -> 0 us
  between operations: 15.1 us -> 0.65 us
    pad x64 -> x0, local copies, waits for them, and re-layouts: 319 us -> none  [scan_pairs(): lax.associative_scan(combine, (decays, additions), axis=0, reverse=backward)]
    add x127 -> x0, other arithmetic: 181 us -> none  [the longest x40 85.6 us: scan_pairs(): lax.associative_scan(combine, (decays, additions), axis=0, reverse=backward)]
    ppermute x64 -> x0, waiting for transfers between devices: 158 us -> none  [passed_along(): lax.ppermute(value, axis, [(source, source + steps) for source in range(l...]
    ppermute x64 -> x0, starting transfers between devices: 147 us -> none  [passed_along(): lax.ppermute(value, axis, [(source, source + steps) for source in range(l...]
    psum x2 -> x0, blocking collectives: 145 us -> none  [the longest x1 119 us: body(): lax.psum((kernel_part, shift_part, bias_part, decay_part, skip_part), 'co...]
    pallas_call x0 -> x2, Pallas kernels: none -> 96.6 us  [the longest x1 94.6 us: layer(): pl.pallas_call(layer_kernel, out_shape=[jax.ShapeDtypeStruct(shape, kind)...]
    unnamed x1 -> x0, blocking collectives: 76 us -> none
    psum x2 -> x0, waiting for transfers between devices: 69.5 us -> none  [the longest x1 69.5 us: body(): projected = lax.psum(partial_proj, 'tensor')]
  transfers between devices with their start and end apart: 77 -> 0, of which waited for: 33 -> 0; matrix products, arithmetic and copies ran while one was open for 6% -> 0% of each run, Pallas kernels for 0% -> 0%
where the time goes in v2:
time: 97.4 us; the launch traced here: 97.2 us
  Pallas kernels  96.6 us (99%)
    pallas_call x1, Pallas kernels, layer(): pl.pallas_call(layer_kernel, out_shape=[jax.ShapeDtypeStruct(shape, kind)...  94.6 us
    pallas_call x1, Pallas kernels, finish(): pl.pallas_call(finish_kernel, out_shape=[jax.ShapeDtypeStruct(shape, BF16...  2.01 us

profile of v2, /device:TPU:1, one launch (start us, length us, event | category | flops | bytes accessed | tf_op | source)
XLA Modules:
  0.0 97.2 jit_solution(14689372614280528378)
XLA Ops:
  0.6 94.6 %layer.1 = (bf16[128,1024]{1,0:T(8,128)(2,1)}, bf16[128,1024]{1,0:T(8,128)(2,1)}, f32[16,1024]{1,0:T(8,128)}, f32[8,128]{1,0:T(8,128)}, f32[16,1024]{1,0:T(8,128)}, /*index=5*/f32[32,8,128]{2,1,0:T(8,128)}) custom-call(bf16[128,1024]{1,0:T(8,128)(2,1)} %refs_0_.1, bf16[128,1024]{1,0:T(8,128)(2,1)} %refs_1_.1, bf16[128,1024]{1,0:T(8,128)(2,1)} %refs_2_.1, ...), custom_call_target="tpu_custom_call" | custom-call | tf_op jit(solution)/shard_map/layer/pallas_call | solution.py:596
  95.2 2.0 %finish.1 = (bf16[128,1024]{1,0:T(8,128)(2,1)}, bf16[128,1024]{1,0:T(8,128)(2,1)}, f32[4,1024]{1,0:T(4,128)}, f32[1,1024]{1,0:T(1,128)}, f32[17,1024]{1,0:T(8,12...) custom-call(bf16[128,1024]{1,0:T(8,128)(2,1)} %get-tuple-element.24.inner_grad, ...), custom_call_target="tpu_custom_call" | custom-call | tf_op jit(solution)/shard_map/finish/pallas_call | solution.py:632

commit v3 on v2

v3 whole, which is shorter than its diff:
```python
import functools

import jax
import jax.numpy as jnp
from jax import lax
from jax.experimental import pallas as pl
from jax.experimental.pallas import tpu as pltpu
from jax.sharding import PartitionSpec as P

N = 16
RANK = 512
TAPS = 4
PROJ = 544
WIDE = 640
T = 128
C = 1024
H = 512
CTX = 32
TEN = 8
CHIPS = CTX // 2
ROWS = T // TEN
LOG2E = 1.4426950408889634
MESH = pl.DeviceIdType.MESH
F32 = jnp.float32
BF16 = jnp.bfloat16
VMEM = pl.BlockSpec(memory_space=pltpu.VMEM)


def dot_nn(a, b):
    return lax.dot_general(a, b, (((1,), (0,)), ((), ())), preferred_element_type=F32)


def dot_nt(a, b):
    return lax.dot_general(a, b, (((1,), (1,)), ((), ())), preferred_element_type=F32)


def dot_tn(a, b):
    return lax.dot_general(a, b, (((0,), (0,)), ((), ())), preferred_element_type=F32)


def iota(shape, axis):
    return lax.broadcasted_iota(jnp.int32, shape, axis)


def sigmoid(v):
    return jax.nn.sigmoid(v)


def silu_slope(v):
    s = sigmoid(v)
    return s * (1.0 + v * (1.0 - s))


def split_tile(v):
    high = v.astype(BF16).astype(F32)
    return jnp.where(iota(v.shape, 1) < 64, high, v - high).astype(BF16)


def far_first(k, size):
    return size // 2 + (k + 1) // 2 * (1 - 2 * lax.rem(k, 2))


class Exchange:
    def __init__(self, src, dst, sems, group, same=False):
        self.src, self.dst, self.send, self.recv = src, dst, sems.at[0], sems.at[1]
        self.group, self.same = group, same
        self.count = {"tensor": TEN, "context": CTX, "chips": CHIPS}[group] - 1

    def copy(self, k):
        if self.group == "tensor":
            at = lax.axis_index("tensor")
            peer = lax.rem(at + far_first(k, TEN), TEN)
            target = {"tensor": peer}
        else:
            me = lax.axis_index("context")
            place, core = (k // 2, 1 - lax.rem(k, 2)) if self.group == "context" else (k, 0)
            x = lax.rem(me // 8 + far_first(place // 4, 4), 4)
            y = lax.rem(me // 2 + far_first(lax.rem(place, 4), 4), 4)
            peer = (x * 4 + y) * 2 + lax.rem(me + core, 2)
            target = {"context": peer}
            at = me
            if self.group == "chips":
                at, peer = me // 2, peer // 2
        return self.made(at, peer, k, target)

    def made(self, at, peer, k, target):
        return pltpu.make_async_remote_copy(
            src_ref=self.src.at[at] if self.same else self.src.at[peer],
            dst_ref=self.dst.at[at],
            send_sem=self.send.at[k],
            recv_sem=self.recv.at[k],
            device_id=target,
            device_id_type=MESH,
        )

    def every(self, act):
        lax.fori_loop(0, self.count, lambda k, _: (act(self.copy(k)), 0)[1], 0)

    def start(self):
        self.every(lambda copy: copy.start())

    def wait_recv(self):
        self.every(lambda copy: copy.wait_recv())

    def wait_send(self):
        self.every(lambda copy: copy.wait_send())

    def to_core(self, core, act):
        other = lax.rem(lax.axis_index("context") + core, 2)
        lax.fori_loop(
            0, CHIPS - 1 + other, lambda q, _: (act(self.copy(2 * q + 1 - other)), 0)[1], 0
        )


class ToEighth(Exchange):
    def __init__(self, src, dst, sems, back=False):
        super().__init__(src, dst, sems, "context")
        self.back = back

    def made(self, at, peer, k, target):
        return pltpu.make_async_remote_copy(
            src_ref=self.src.at[at // 4 if self.back else peer // 4],
            dst_ref=self.dst.at[at // 4 if self.back else at],
            send_sem=self.send.at[k],
            recv_sem=self.recv.at[k],
            device_id=target,
            device_id_type=MESH,
        )

    def few(self, act):
        me = lax.axis_index("context")
        odd = lax.rem(me // 2, 2)

        def one(m, _):
            b = lax.rem(m, 2) * (3 - 2 * odd) + odd
            act(self.copy(2 * (m // 2 * 4 + b) + 1 - lax.rem(me, 2)))
            return 0

        lax.fori_loop(0, 8 - lax.rem(me + 3, 4) // 3, one, 0)

    def all(self, act):
        @pl.when(lax.rem(lax.axis_index("context"), 4) == 0)
        def _():
            self.every(act)

    def start(self):
        (self.all if self.back else self.few)(lambda copy: copy.start())

    def wait_recv(self):
        (self.few if self.back else self.all)(lambda copy: copy.wait_recv())

    def wait_send(self):
        (self.all if self.back else self.few)(lambda copy: copy.wait_send())


def greet(axis, size):
    me = lax.axis_index(axis)
    barrier = pltpu.get_barrier_semaphore()

    def signal(off, _):
        pl.semaphore_signal(
            barrier, inc=1, device_id={axis: lax.rem(me + off, size)}, device_id_type=MESH
        )
        return 0

    lax.fori_loop(1, size, signal, 0)


def to_neighbour(src, dst, send, recv, step):
    peer = lax.rem(lax.axis_index("context") + step + CTX, CTX)
    return pltpu.make_async_remote_copy(
        src_ref=src, dst_ref=dst, send_sem=send, recv_sem=recv,
        device_id={"context": peer}, device_id_type=MESH,
    )


def spread(z, tile):
    rows = T * N
    repeat = (iota((rows, T), 0) // N == iota((rows, T), 1)).astype(BF16)
    each = dot_nn(repeat, tile)
    place = iota((rows, 128), 1) % 64 - iota((rows, 128), 0) % N
    unit = jnp.ones((128, 128), BF16)
    z.bspread[...] = dot_nn(jnp.where(place == 0, each, 0.0).astype(BF16), unit).reshape(T, N, 128)
    z.cspread[...] = dot_nn(jnp.where(place == N, each, 0.0).astype(BF16), unit).reshape(T, N, 128)


HALVES = C // H
LT = H // 128

SCRATCH = (
    ("pad", (T + 16, C), F32),
    ("pre", (T, C), F32),
    ("conv", (T, C), F32),
    ("slope", (T, C), F32),
    ("half", (T, C), BF16),
    ("ocot", (T, C), F32),
    ("gslope", (T, C), F32),
    ("sig", (T, C), F32),
    ("deltas", (T, C), F32),
    ("dx", (T, C), F32),
    ("y", (T + 16, C), F32),
    ("along", (T + 16, C), F32),
    ("wsum", (T + 16, C), F32),
    ("direct", (T, C), F32),
    ("halo", (16, C), BF16),
    ("wtail", (128, C), BF16),
    ("part", (TEN, ROWS, WIDE), BF16),
    ("got_part", (TEN, ROWS, WIDE), BF16),
    ("proj", (TEN, ROWS, WIDE), BF16),
    ("bspread", (T, N, 128), F32),
    ("cspread", (T, N, 128), F32),
    ("bblock", (T, 16 * N), BF16),
    ("cblock", (T, 16 * N), BF16),
    ("steps", (CTX, 8, 128), F32),
    ("ends", (CTX, 8, 128), F32),
    ("got_ends", (CTX, 8, 128), F32),
    ("decays", (CTX, 8, 128), F32),
    ("back", (CTX, 8, 128), F32),
    ("borders", (CTX, 8, 128), F32),
    ("before", (T, N, H), F32),
    ("isum", (HALVES, T, N, 128), F32),
    ("osum", (HALVES, T, N, 128), F32),
    ("work0", (16 * N, H), BF16),
    ("work1", (16 * N, H), BF16),
    ("rates0", (16 * N, H), BF16),
    ("rates1", (16 * N, H), BF16),
    ("decay_part", (N, C), F32),
    ("psel", (TEN, ROWS, WIDE), BF16),
    ("got_psel", (TEN, ROWS, WIDE), BF16),
    ("sel", (TEN, ROWS, WIDE), BF16),
    ("order", (WIDE, WIDE), BF16),
    ("fold", (T, T * N), BF16),
    ("dterm", (HALVES, 2, CHIPS, 16, H), BF16),
    ("dpair", (HALVES, CHIPS, 16, H), BF16),
    ("dsum", (HALVES, CHIPS, 16, H), BF16),
    ("got_d", (HALVES, CHIPS, 16, H), BF16),
    ("mterm", (2, CHIPS, 16, C), BF16),
    ("mpair", (CHIPS, 16, C), BF16),
    ("msum", (CHIPS, 16, C), BF16),
    ("got_m", (CHIPS, 16, C), BF16),
    ("own", (CTX, 8, 128), F32),
    ("got_own", (CTX, 8, 128), F32),
    ("extra", (CTX, 8, 128), F32),
    ("got_extra", (CTX, 8, 128), F32),
    ("last", (8, 8, 128), F32),
    ("got_last", (CTX, 8, 128), F32),
    ("trail", (T + 8, C), F32),
    ("edge", (8, C), F32),
    ("late", (8, C), F32),
)
INPUTS = (
    ("inner", (T, C), BF16),
    ("gate", (T, C), BF16),
    ("grad", (T, C), BF16),
    ("taps", (TAPS, C), F32),
    ("shift", (1, C), F32),
    ("wsel", (PROJ, C), BF16),
    ("wdelta", (C, RANK), BF16),
    ("bias", (1, C), F32),
    ("dlog", (N, C), F32),
    ("skip", (1, C), F32),
)
OUTPUTS = (
    ("inner_grad", (T, C), BF16),
    ("gate_grad", (T, C), BF16),
    ("sel_main", (16, C), F32),
    ("sel_extra", (8, 128), F32),
    ("delta_grad", (16, C), F32),
    ("params", (CTX, 8, 128), F32),
    ("late_params", (8, 8, 128), F32),
)
SEMS = (
    ("in", (len(INPUTS),)),
    ("halo", (2,)),
    ("part", (2, TEN)),
    ("proj", (2, TEN)),
    ("steps", (2, CTX)),
    ("ends", (2, CTX)),
    ("back", (2, CTX)),
    ("psel", (2, TEN)),
    ("sel", (2, TEN)),
    ("dpair", (HALVES, 2)),
    ("dsum", (HALVES, 2, CHIPS)),
    ("mpair", (2,)),
    ("msum", (2, CHIPS)),
    ("own", (2, CTX)),
    ("params", (2, CTX)),
    ("extra", (2, CTX)),
    ("last", (2, CTX)),
    ("spread", (2, CTX)),
    ("edge", (2,)),
)


class Refs:
    pass


def tile_of(v, r, k):
    return v[8 * r : 8 * r + 8, 128 * k : 128 * k + 128]


def wide_of(v):
    return jnp.concatenate([v] * LT, 1)


def lane_sum(v):
    return functools.reduce(jnp.add, [v[:, 128 * k : 128 * k + 128] for k in range(LT)])


def half_lanes(h):
    return pl.ds(pl.multiple_of(h * H, H), H)


def rows_of(block):
    return pl.ds(pl.multiple_of(block * 16, 16), 16)


def convolve(z, first, rows):
    value = jnp.zeros((rows, C), F32) + z.shift[...]
    for k in range(TAPS):
        value = value + z.taps[k : k + 1, :] * z.pad[pl.ds(first + 16 - TAPS + 1 + k, rows), :]
    z.pre[pl.ds(first, rows), :] = value
    s = sigmoid(value)
    conv = value * s
    z.conv[pl.ds(first, rows), :] = conv
    z.half[pl.ds(first, rows), :] = conv.astype(BF16)
    z.slope[pl.ds(first, rows), :] = s * (1.0 + value * (1.0 - s))


def project(z, first, rows):
    half = z.half[pl.ds(first, rows), :]
    blocks = pl.ds(first // ROWS, rows // ROWS)
    shape = (rows // ROWS, ROWS)
    z.part[blocks, :, :RANK] = dot_nt(half, z.wsel[:RANK, :]).astype(BF16).reshape(*shape, RANK)
    z.part[blocks, :, RANK:] = split_tile(dot_nt(half, z.wtail[...])).reshape(*shape, 128)


def border_at(direction, r, k, h):
    return (direction * 8 + r * LT + k) * 2 + h


def summarize(z, h):
    lanes = slice(h * H, h * H + H)
    rate = jnp.exp(z.dlog[:, lanes]) * (-LOG2E)

    def steps(block, carried):
        state, decay, flow = carried
        for i in range(8):
            t = block * 8 + i
            row = pl.ds(t, 1)
            d = jnp.exp2(z.deltas[row, lanes] * rate)
            state = d * state + z.dx[row, lanes] * wide_of(z.bspread[t])
            decay = decay * d
            flow = flow + decay * (z.ocot[row, lanes] * wide_of(z.cspread[t]))
        return state, decay, flow

    zero = jnp.zeros((N, H), F32)
    state, _, flow = lax.fori_loop(0, T // 8, steps, (zero, zero + 1.0, zero))
    for r in range(N // 8):
        for k in range(LT):
            z.ends[border_at(0, r, k, h)] = tile_of(state, r, k)
            z.ends[border_at(1, r, k, h)] = tile_of(flow, r, k)


def edges(z, direction, h):
    return jnp.concatenate(
        [
            jnp.concatenate([z.borders[border_at(direction, r, k, h)] for k in range(LT)], 1)
            for r in range(N // 8)
        ],
        0,
    )


def ones_block():
    return (iota((16, 16 * N), 0) == iota((16, 16 * N), 1) // N).astype(BF16)


def go_forward(z, h):
    lanes = slice(h * H, h * H + H)
    rate2 = jnp.exp(z.dlog[:, lanes]) * (-LOG2E)
    works = (z.work0, z.work1)
    z.work1[...] = jnp.zeros((16 * N, H), BF16)

    def reduce(block, work):
        z.y[rows_of(block + 1), lanes] = dot_nn(z.cblock[rows_of(jnp.maximum(block, 0)), :], work[...])

    def pair(index, state):
        for p in range(2):
            block = index * 2 + p
            reduce(block - 1, works[1 - p])
            for i in range(16):
                t = block * 16 + i
                row = pl.ds(t, 1)
                z.before[t] = state
                d = jnp.exp2(z.deltas[row, lanes] * rate2)
                state = d * state + z.dx[row, lanes] * wide_of(z.bspread[t])
                works[p][N * i : N * i + N, :] = state.astype(BF16)
                z.osum[h, t] = lane_sum(state * z.ocot[row, lanes])
        return state

    lax.fori_loop(0, T // 32, pair, edges(z, 0, h))
    reduce(T // 16 - 1, z.work1)


def go_backward(z, h):
    lanes = slice(h * H, h * H + H)
    rate = -jnp.exp(z.dlog[:, lanes])
    rate2 = rate * LOG2E
    ones = ones_block()
    works, rates = (z.work0, z.work1), (z.rates0, z.rates1)
    z.work0[...] = jnp.zeros((16 * N, H), BF16)
    z.rates0[...] = jnp.zeros((16 * N, H), BF16)

    def reduce(block, work, rated):
        rows = rows_of(block)
        z.along[rows, lanes] = dot_nn(z.bblock[rows_of(jnp.minimum(block, T // 16 - 1)), :], work[...])
        z.wsum[rows, lanes] = dot_nn(ones, rated[...])

    def pair(index, carried):
        flow, total = carried
        for p in reversed(range(2)):
            block = T // 16 - 2 - index * 2 + p
            reduce(block + 1, works[1 - p], rates[1 - p])
            for i in reversed(range(16)):
                t = block * 16 + i
                row = pl.ds(t, 1)
                delta = z.deltas[row, lanes]
                adjoint = z.ocot[row, lanes] * wide_of(z.cspread[t]) + flow
                z.isum[h, t] = lane_sum(adjoint * z.dx[row, lanes])
                works[p][N * i : N * i + N, :] = adjoint.astype(BF16)
                flow = jnp.exp2(delta * rate2) * adjoint
                weighted = flow * z.before[t]
                total = total + weighted * delta
                rates[p][N * i : N * i + N, :] = (weighted * rate).astype(BF16)
        return flow, total

    _, total = lax.fori_loop(0, T // 32, pair, (edges(z, 1, h), jnp.zeros((N, H), F32)))
    reduce(0, z.work0, z.rates0)
    z.decay_part[:, lanes] = total * rate


def gather_sums(z):
    unit = jnp.ones((128, 128), BF16)
    place = iota((T * N, 128), 1) - iota((T * N, 128), 0) % N

    def summed(parts):
        return dot_nn((parts[0] + parts[1]).reshape(T * N, 128).astype(BF16), unit)

    both = jnp.where(
        place == 0, summed(z.isum), jnp.where(place == N, summed(z.osum), 0.0)
    ).astype(BF16)
    z.psel[:, :, RANK:] = dot_nn(z.fold[...], both).astype(BF16).reshape(TEN, ROWS, 128)


def to_sibling(src, dst, sems):
    me = lax.axis_index("context")
    return pltpu.make_async_remote_copy(
        src_ref=src, dst_ref=dst, send_sem=sems.at[0], recv_sem=sems.at[1],
        device_id={"context": me + 1 - 2 * lax.rem(me, 2)}, device_id_type=MESH,
    )


def send_deltas(z, sem, h, pair):
    chip, core = lax.axis_index("context") // 2, lax.rem(lax.axis_index("context"), 2)
    pair.wait()
    z.dsum[h] = (z.dterm[h, core].astype(F32) + z.dpair[h].astype(F32)).astype(BF16)
    sent = Exchange(
        z.dsum.at[h], z.got_d.at[h], sem.dsum.at[h], "chips"
    )
    sent.start()
    z.got_d[h, chip] = z.dsum[h, chip]
    return sent


def layer_kernel(*refs):
    z, given, sem = Refs(), Refs(), Refs()
    refs = list(refs)
    for name, _, _ in INPUTS:
        setattr(given, name, refs.pop(0))
    for name, _, _ in OUTPUTS + INPUTS + SCRATCH:
        setattr(z, name, refs.pop(0))
    for name, _ in SEMS:
        setattr(sem, name, refs.pop(0))
    ctx, ten = lax.axis_index("context"), lax.axis_index("tensor")
    chip, core = ctx // 2, lax.rem(ctx, 2)

    loads = {}
    for i, (name, _, _) in enumerate(INPUTS):
        loads[name] = pltpu.make_async_copy(
            getattr(given, name), getattr(z, name), getattr(sem, "in").at[i]
        )

    for name in ("inner", "taps", "shift", "wsel", "gate", "grad", "dlog", "wdelta", "bias", "skip"):
        loads[name].start()
    greet("tensor", TEN)
    greet("context", CTX)

    for name in ("inner", "taps", "shift"):
        loads[name].wait()
    z.pad[16:, :] = z.inner[...].astype(F32)
    convolve(z, 16, T - 16)
    pl.semaphore_wait(pltpu.get_barrier_semaphore(), TEN - 1 + CTX - 1)
    halo = to_neighbour(z.inner.at[pl.ds(T - 16, 16)], z.halo, sem.halo.at[0], sem.halo.at[1], 1)
    halo.start()
    loads["wsel"].wait()
    tail = z.wsel[RANK:PROJ, :]
    z.wtail[0:32, :] = tail
    z.wtail[32:64, :] = jnp.zeros((32, C), BF16)
    z.wtail[64:96, :] = tail
    z.wtail[96:128, :] = jnp.zeros((32, C), BF16)
    project(z, 16, T - 16)
    halo.wait()
    z.pad[0:16, :] = z.halo[...].astype(F32) * (ctx > 0).astype(F32)
    convolve(z, 0, 16)
    project(z, 0, 16)
    scatter = Exchange(z.part, z.got_part, sem.part, "tensor")
    scatter.start()
    z.got_part[ten] = z.part[ten]

    loads["gate"].wait()
    loads["grad"].wait()
    g = z.gate[...].astype(F32)
    s = sigmoid(g)
    grad = z.grad[...].astype(F32)
    z.ocot[...] = grad * (g * s)
    z.gslope[...] = grad * (s * (1.0 + g * (1.0 - s)))

    scatter.wait_recv()
    total = jnp.sum(z.got_part[...].astype(F32), axis=0)
    bc = total[:, RANK:]
    bc = bc + pltpu.roll(bc, 64, 1)
    z.proj[ten, :, :RANK] = total[:, :RANK].astype(BF16)
    z.proj[ten, :, RANK:] = split_tile(bc)
    gather = Exchange(
        z.proj, z.proj, sem.proj, "tensor", same=True
    )
    gather.start()
    target = iota((WIDE, WIDE), 0)
    source = iota((WIDE, WIDE), 1)
    place = target % 256
    order = jnp.where(
        target < RANK,
        (place // 16 * 2 + target // 256) * 17 + place % 16,
        (target - RANK) * 17 + 16,
    )
    z.order[...] = ((order == source) & (target < PROJ)).astype(BF16)
    z.fold[...] = (iota((T, T * N), 0) == iota((T, T * N), 1) // N).astype(BF16)
    for name in ("dlog", "wdelta", "bias", "skip"):
        loads[name].wait()
    gather.wait_recv()

    flat = z.proj[...].reshape(T, WIDE)
    raw = dot_nt(flat[:, :RANK], z.wdelta[...]) + z.bias[...]
    step = jnp.maximum(raw, 0.0) + jnp.log1p(jnp.exp(-jnp.abs(raw)))
    z.deltas[...] = step
    lengths = jnp.sum(step, axis=0, keepdims=True)
    for k in range(8):
        z.steps[ctx, k : k + 1, :] = lengths[:, 128 * k : 128 * k + 128]
    steps = Exchange(
        z.steps, z.steps, sem.steps, "context", same=True
    )
    steps.start()
    z.sig[...] = sigmoid(raw)
    z.dx[...] = step * z.conv[...]
    spread(z, flat[:, RANK:])
    ends = Exchange(z.ends, z.got_ends, sem.ends, "context")
    for h in range(HALVES):
        summarize(z, h)
        ends.to_core(h, lambda copy: copy.start())

    z.got_ends[ctx] = z.ends[ctx]
    backward = chip // 8
    at_row = pl.ds(pl.multiple_of(lax.rem(chip, 8) // LT * 8, 8), 8)
    at_lane = core * LT + lax.rem(chip, LT)
    rate = jnp.exp(z.dlog[at_row, pl.ds(pl.multiple_of(at_lane * 128, 128), 128)]) * (-LOG2E)
    steps.wait_recv()

    def shrink(i, _):
        z.decays[i] = jnp.exp2(rate * z.steps[i, pl.ds(at_lane, 1), :])
        return 0

    lax.fori_loop(0, CTX, shrink, 0)
    column = iota((128, 16 * N), 1)
    same = iota((T, 16 * N), 0) % 16 == column // N
    lane = iota((128, 16 * N), 0) % 64
    z.bblock[...] = jnp.where(
        same, dot_nn(flat[:, RANK:], (lane == column % N).astype(BF16)), 0.0
    ).astype(BF16)
    z.cblock[...] = jnp.where(
        same, dot_nn(flat[:, RANK:], (lane == column % N + N).astype(BF16)), 0.0
    ).astype(BF16)
    ends.wait_recv()

    def follow(i, carried):
        at = i + backward * (CTX - 1 - 2 * i)
        z.back[at] = carried
        return z.decays[at] * carried + z.got_ends[at]

    lax.fori_loop(0, CTX, follow, jnp.zeros((8, 128), F32))
    home = Exchange(z.back, z.borders, sem.back, "context")
    home.start()
    z.borders[ctx] = z.back[ctx]
    scatter.wait_send()
    gather.wait_send()
    steps.wait_send()

    rank_part = jnp.zeros((T, RANK), F32)
    dpairs, deltas, sides = [], [], []
    for h in range(HALVES):
        lanes = slice(h * H, h * H + H)
        home.to_core(h, lambda copy: copy.wait_recv())
        go_forward(z, h)
        if h > 0:
            deltas.append(send_deltas(z, sem, h - 1, dpairs[h - 1]))
        go_backward(z, h)
        near = z.along[0:T, lanes]
        raw_cot = (z.wsum[0:T, lanes] + z.conv[:, lanes] * near) * z.sig[:, lanes]
        raw_half = raw_cot.astype(BF16)
        rank_part = rank_part + dot_nn(raw_half, z.wdelta[lanes, :])
        if h == HALVES - 1:
            gather_sums(z)
            z.psel[:, :, :RANK] = rank_part.astype(BF16).reshape(TEN, ROWS, RANK)
            scatter2 = Exchange(z.psel, z.got_psel, sem.psel, "tensor")
            scatter2.start()
            z.got_psel[ten] = z.psel[ten]
        term = dot_tn(flat[:, :RANK], raw_half).astype(BF16).reshape(CHIPS, 2, 16, H)
        z.dterm[h, 0] = term[:, 0]
        z.dterm[h, 1] = term[:, 1]
        dpairs.append(to_sibling(z.dterm.at[h, 1 - core], z.dpair.at[h], sem.dpair.at[h]))
        dpairs[h].start()
        cot, gain, conv = z.ocot[:, lanes], z.skip[:, lanes], z.conv[:, lanes]
        z.gate_grad[:, lanes] = (
            z.gslope[:, lanes] * (z.y[16 : T + 16, lanes] + gain * conv)
        ).astype(BF16)
        z.direct[:, lanes] = gain * cot + z.deltas[:, lanes] * near
        sides.append(
            jnp.concatenate(
                [
                    jnp.sum(raw_cot, axis=0, keepdims=True),
                    jnp.sum(cot * conv, axis=0, keepdims=True),
                    jnp.zeros((6, H), F32),
                ],
                0,
            )
        )

    scatter2.wait_recv()
    z.sel[ten] = jnp.sum(z.got_psel[...].astype(F32), axis=0).astype(BF16)
    gather2 = Exchange(z.sel, z.sel, sem.sel, "tensor", same=True)
    gather2.start()
    deltas.append(send_deltas(z, sem, HALVES - 1, dpairs[HALVES - 1]))
    early = jnp.concatenate(sides, 1)
    for k in range(8):
        lanes = slice(128 * k, 128 * k + 128)
        z.own[k] = z.decay_part[0:8, lanes]
        z.own[8 + k] = z.decay_part[8:16, lanes]
        z.own[16 + k] = early[:, lanes]
        z.own[24 + k] = jnp.zeros((8, 128), F32)
    sums = Exchange(z.own, z.got_own, sem.own, "context")
    sums.start()
    z.got_own[ctx] = z.own[ctx]
    gather2.wait_recv()
    select_cot = z.sel[...].reshape(T, WIDE)

    turned = dot_nt(z.order[...], select_cot).astype(BF16)
    z.mterm[...] = dot_nn(turned[:RANK, :], z.half[...]).astype(BF16).reshape(2, CHIPS, 16, C)
    mpair = to_sibling(z.mterm.at[1 - core], z.mpair, sem.mpair)
    mpair.start()
    pre_cot = (z.direct[...] + dot_nn(select_cot[:, :PROJ], z.wsel[...])) * z.slope[...]
    z.trail[0:T, :] = pre_cot
    z.edge[...] = pre_cot[0:8, :]
    below = to_neighbour(z.edge, z.late, sem.edge.at[0], sem.edge.at[1], -1)
    below.start()
    rows = [jnp.sum(pre_cot, axis=0, keepdims=True)]
    for k in range(TAPS):
        rows.append(
            jnp.sum(pre_cot * z.pad[pl.ds(16 - TAPS + 1 + k, T), :], axis=0, keepdims=True)
        )
    rows = jnp.concatenate(rows + [jnp.zeros((3, C), F32)], 0)
    for k in range(8):
        z.last[k] = rows[:, 128 * k : 128 * k + 128]
    lasts = ToEighth(z.last, z.got_last, sem.last)
    lasts.start()
    z.got_last[ctx] = z.last[ctx // 4]
    mpair.wait()
    z.msum[...] = (z.mterm[core].astype(F32) + z.mpair[...].astype(F32)).astype(BF16)
    mains = Exchange(
        z.msum, z.got_m, sem.msum, "chips"
    )
    mains.start()
    z.got_m[chip] = z.msum[chip]
    sums.wait_recv()
    z.params[ctx] = jnp.sum(z.got_own[...], axis=0)
    spreads = Exchange(
        z.params, z.params, sem.params, "context", same=True
    )
    spreads.start()
    extra = dot_nn(turned[RANK : RANK + CTX, :], z.half[...])
    for k in range(8):
        z.extra[:, k, :] = extra[:, 128 * k : 128 * k + 128]
    extras = Exchange(z.extra, z.got_extra, sem.extra, "context")
    extras.start()
    z.got_extra[ctx] = z.extra[ctx]

    below.wait()
    z.trail[T:, :] = z.late[...] * (ctx < CTX - 1).astype(F32)
    result = jnp.zeros((T, C), F32)
    for k in range(TAPS):
        result = result + z.taps[k : k + 1, :] * z.trail[pl.ds(TAPS - 1 - k, T), :]
    z.inner_grad[...] = result.astype(BF16)

    lasts.wait_recv()

    @pl.when(lax.rem(ctx, 4) == 0)
    def _():
        z.late_params[ctx // 4] = jnp.sum(z.got_last[...], axis=0)

    shares = ToEighth(
        z.late_params, z.late_params, sem.spread, back=True
    )
    shares.start()
    for h in range(HALVES):
        deltas[h].wait_recv()
        z.delta_grad[:, h * H : h * H + H] = jnp.sum(z.got_d[h].astype(F32), axis=0)
    for exchange in (ends, home, scatter2, gather2, sums, deltas[0], deltas[1]):
        exchange.wait_send()
    extras.wait_recv()
    z.sel_extra[...] = jnp.sum(z.got_extra[...], axis=0)
    mains.wait_recv()
    z.sel_main[...] = jnp.sum(z.got_m[...].astype(F32), axis=0)
    spreads.wait_recv()
    shares.wait_recv()
    for exchange in (lasts, mains, spreads, extras, shares):
        exchange.wait_send()


def layer(*args):
    return pl.pallas_call(
        layer_kernel,
        out_shape=[jax.ShapeDtypeStruct(shape, kind) for _, shape, kind in OUTPUTS],
        in_specs=[pl.BlockSpec(memory_space=pl.ANY)] * len(INPUTS),
        out_specs=[VMEM] * len(OUTPUTS),
        scratch_shapes=[pltpu.VMEM(shape, kind) for _, shape, kind in INPUTS + SCRATCH]
        + [pltpu.SemaphoreType.DMA(shape) for _, shape in SEMS],
        compiler_params=pltpu.CompilerParams(
            collective_id=0, has_side_effects=True, vmem_limit_bytes=56 << 20
        ),
        name="layer",
    )(*args)


def finish_kernel(
    inner_grad, gate_grad, sel_main, sel_extra, delta, params, late,
    inner_out, gate_out, taps_out, shift_out, sel_out, delta_out, bias_out, decay_out, skip_out,
):
    inner_out[...] = inner_grad[...]
    gate_out[...] = gate_grad[...]
    sel_out[0:16, :] = sel_main[...]
    delta_out[...] = delta[...]
    for k in range(8):
        lanes = slice(128 * k, 128 * k + 128)
        sel_out[16:17, lanes] = sel_extra[k : k + 1, :]
        decay_out[0:8, lanes] = params[k]
        decay_out[8:16, lanes] = params[8 + k]
        rows = params[16 + k]
        bias_out[:, lanes] = rows[0:1, :]
        skip_out[:, lanes] = rows[1:2, :]
        shift_out[:, lanes] = late[k, 0:1, :]
        taps_out[:, lanes] = late[k, 1:5, :]


def finish(*args):
    shapes = ((T, C), (T, C), (TAPS, C), (1, C), (17, C), (16, C), (1, C), (N, C), (1, C))
    return pl.pallas_call(
        finish_kernel,
        out_shape=[
            jax.ShapeDtypeStruct(shape, BF16 if i < 2 else F32) for i, shape in enumerate(shapes)
        ],
        in_specs=[VMEM] * 7,
        out_specs=[VMEM] * 9,
        name="finish",
    )(*args)


def body(
    inner_in, gate_in, out_grad, kernel, kernel_shift, select_proj, delta_proj, delta_bias,
    decay_log, skip_gain,
):
    parts = layer(
        inner_in, gate_in, out_grad, kernel.T, kernel_shift[None], select_proj, delta_proj,
        delta_bias[None], decay_log.T, skip_gain[None],
    )
    inner_grad, gate_grad, taps, shift, select, delta, bias, decay, skip = finish(*parts)
    return (
        inner_grad, gate_grad, taps.T, shift[0], select, delta.T, bias[0], decay.T, skip[0],
    )


def solution(mesh):
    return jax.shard_map(
        body,
        mesh=mesh,
        in_specs=(
            P("context", "tensor"),
            P("context", "tensor"),
            P("context", "tensor"),
            P("tensor", None),
            P("tensor"),
            P(None, "tensor"),
            P("tensor", None),
            P("tensor"),
            P("tensor", None),
            P("tensor"),
        ),
        out_specs=(
            P("context", "tensor"),
            P("context", "tensor"),
            P("tensor", None),
            P("tensor"),
            P("context", "tensor"),
            P("tensor", "context"),
            P("tensor"),
            P("tensor", None),
            P("tensor"),
        ),
        check_vma=False,
    )
```

time: 97.4 us -> 89 us (0.914)
  Pallas kernels: 96.6 us -> 88.2 us
    pallas_call x1, Pallas kernels: 94.6 us -> 86.2 us  [layer(): pl.pallas_call(layer_kernel, out_shape=[jax.ShapeDtypeStruct(shape, kind)...]
where the time goes in v3:
time: 89 us; the launch traced here: 88.9 us
  Pallas kernels  88.2 us (99%)
    pallas_call x1, Pallas kernels, layer(): pl.pallas_call(layer_kernel, out_shape=[jax.ShapeDtypeStruct(shape, kind)...  86.2 us
    pallas_call x1, Pallas kernels, finish(): pl.pallas_call(finish_kernel, out_shape=[jax.ShapeDtypeStruct(shape, BF16...  1.99 us

profile of v3, /device:TPU:1, one launch (start us, length us, event | category | flops | bytes accessed | tf_op | source)
XLA Modules:
  0.0 88.9 jit_solution(15358223541103064020)
XLA Ops:
  0.6 86.2 %layer.1 = (bf16[128,1024]{1,0:T(8,128)(2,1)}, bf16[128,1024]{1,0:T(8,128)(2,1)}, f32[16,1024]{1,0:T(8,128)}, f32[8,128]{1,0:T(8,128)}, f32[16,1024]{1,0:T(8,128...) custom-call(bf16[128,1024]{1,0:T(8,128)(2,1)} %refs_0_.1, bf16[128,1024]{1,0:T(8,128)(2,1)} %refs_1_.1, ...), custom_call_target="tpu_custom_call" | custom-call | tf_op jit(solution)/shard_map/layer/pallas_call | solution.py:740
  86.9 2.0 %finish.1 = (bf16[128,1024]{1,0:T(8,128)(2,1)}, bf16[128,1024]{1,0:T(8,128)(2,1)}, f32[4,1024]{1,0:T(4,128)}, f32[1,1024]{1,0:T(1,128)}, f32[17,1024]{1,0:T(8,12...) custom-call(bf16[128,1024]{1,0:T(8,128)(2,1)} %get-tuple-element.25.inner_grad, ...), custom_call_target="tpu_custom_call" | custom-call | tf_op jit(solution)/shard_map/finish/pallas_call | solution.py:776

commit v4 on v3

v4 whole, which is shorter than its diff:
```python
import functools

import jax
import jax.numpy as jnp
from jax import lax
from jax.experimental import pallas as pl
from jax.experimental.pallas import tpu as pltpu
from jax.sharding import PartitionSpec as P

N = 16
RANK = 512
TAPS = 4
PROJ = 544
WIDE = 640
T = 128
C = 1024
H = 512
CTX = 32
TEN = 8
CHIPS = CTX // 2
ROWS = T // TEN
LOG2E = 1.4426950408889634
MESH = pl.DeviceIdType.MESH
F32 = jnp.float32
BF16 = jnp.bfloat16
VMEM = pl.BlockSpec(memory_space=pltpu.VMEM)


def dot_nn(a, b):
    return lax.dot_general(a, b, (((1,), (0,)), ((), ())), preferred_element_type=F32)


def dot_nt(a, b):
    return lax.dot_general(a, b, (((1,), (1,)), ((), ())), preferred_element_type=F32)


def dot_tn(a, b):
    return lax.dot_general(a, b, (((0,), (0,)), ((), ())), preferred_element_type=F32)


def iota(shape, axis):
    return lax.broadcasted_iota(jnp.int32, shape, axis)


def sigmoid(v):
    return jax.nn.sigmoid(v)


def silu_slope(v):
    s = sigmoid(v)
    return s * (1.0 + v * (1.0 - s))


def split_tile(v):
    high = v.astype(BF16).astype(F32)
    return jnp.where(iota(v.shape, 1) < 64, high, v - high).astype(BF16)


def far_first(k, size):
    if isinstance(k, int):
        return size // 2 + (k + 1) // 2 * (1 - 2 * (k % 2))
    return size // 2 + (k + 1) // 2 * (1 - 2 * lax.rem(k, 2))


def peer_of(group, k):
    if group == "tensor":
        at = lax.axis_index("tensor")
        peer = lax.rem(at + far_first(k, TEN), TEN)
        return at, peer, {"tensor": peer}
    me = lax.axis_index("context")
    place, core = (k // 2, 1 - k % 2) if group == "context" else (k, 0)
    x = lax.rem(me // 8 + far_first(place // 4, 4), 4)
    y = lax.rem(me // 2 + far_first(place % 4, 4), 4)
    peer = (x * 4 + y) * 2 + lax.rem(me + core, 2)
    if group == "chips":
        return me // 2, x * 4 + y, {"context": peer}
    return me, peer, {"context": peer}


PEERS = {"tensor": TEN - 1, "context": CTX - 1, "chips": CHIPS - 1}


class Exchange:
    def __init__(self, src, dst, sems, group, same=False):
        self.src, self.dst, self.send, self.recv = src, dst, sems.at[0], sems.at[1]
        self.group, self.same = group, same

    def copy(self, k):
        at, peer, target = peer_of(self.group, k)
        return pltpu.make_async_remote_copy(
            src_ref=self.src.at[at] if self.same else self.src.at[peer],
            dst_ref=self.dst.at[at],
            send_sem=self.send.at[k],
            recv_sem=self.recv.at[k],
            device_id=target,
            device_id_type=MESH,
        )

    def every(self, act):
        lax.fori_loop(0, PEERS[self.group], lambda k, _: (act(self.copy(k)), 0)[1], 0)

    def start(self):
        for k in range(PEERS[self.group]):
            self.copy(k).start()

    def wait_recv(self):
        self.every(lambda copy: copy.wait_recv())

    def wait_send(self):
        self.every(lambda copy: copy.wait_send())

    def to_core(self, core, act):
        other = lax.rem(lax.axis_index("context") + core, 2)
        lax.fori_loop(
            0, CHIPS - 1 + other, lambda q, _: (act(self.copy(2 * q + 1 - other)), 0)[1], 0
        )


def greet(group):
    barrier = pltpu.get_barrier_semaphore()

    for k in range(PEERS[group]):
        pl.semaphore_signal(barrier, inc=1, device_id=peer_of(group, k)[2], device_id_type=MESH)


def to_neighbour(src, dst, send, recv, step):
    peer = lax.rem(lax.axis_index("context") + step + CTX, CTX)
    return pltpu.make_async_remote_copy(
        src_ref=src, dst_ref=dst, send_sem=send, recv_sem=recv,
        device_id={"context": peer}, device_id_type=MESH,
    )


def spread(z, tile):
    rows = T * N
    repeat = (iota((rows, T), 0) // N == iota((rows, T), 1)).astype(BF16)
    each = dot_nn(repeat, tile)
    place = iota((rows, 128), 1) % 64 - iota((rows, 128), 0) % N
    unit = jnp.ones((128, 128), BF16)
    z.bspread[...] = dot_nn(jnp.where(place == 0, each, 0.0).astype(BF16), unit).reshape(T, N, 128)
    z.cspread[...] = dot_nn(jnp.where(place == N, each, 0.0).astype(BF16), unit).reshape(T, N, 128)


HALVES = C // H
LT = H // 128

SCRATCH = (
    ("pad", (T + 16, C), F32),
    ("pre", (T, C), F32),
    ("conv", (T, C), F32),
    ("slope", (T, C), F32),
    ("half", (T, C), BF16),
    ("ocot", (T, C), F32),
    ("gslope", (T, C), F32),
    ("sig", (T, C), F32),
    ("deltas", (T, C), F32),
    ("dx", (T, C), F32),
    ("y", (T, C), F32),
    ("along", (T, C), F32),
    ("wsum", (T, C), F32),
    ("direct", (T, C), F32),
    ("halo", (16, C), BF16),
    ("wtail", (128, C), BF16),
    ("part", (TEN, ROWS, WIDE), BF16),
    ("got_part", (TEN, ROWS, WIDE), BF16),
    ("proj", (TEN, ROWS, WIDE), BF16),
    ("bspread", (T, N, 128), F32),
    ("cspread", (T, N, 128), F32),
    ("ends", (CTX, 9, 128), F32),
    ("got_ends", (CTX, 9, 128), F32),
    ("decays", (CTX, 8, 128), F32),
    ("back", (CTX, 8, 128), F32),
    ("borders", (CTX, 8, 128), F32),
    ("before", (T, N, H), F32),
    ("isum", (HALVES, T, N, 128), F32),
    ("osum", (HALVES, T, N, 128), F32),
    ("decay_part", (N, C), F32),
    ("psel", (TEN, ROWS, WIDE), BF16),
    ("got_psel", (TEN, ROWS, WIDE), BF16),
    ("sel", (TEN, ROWS, WIDE), BF16),
    ("order", (WIDE, WIDE), BF16),
    ("fold", (T, T * N), BF16),
    ("dterm", (HALVES, 2, CHIPS, 16, H), BF16),
    ("dpair", (HALVES, CHIPS, 16, H), BF16),
    ("dsum", (HALVES, CHIPS, 16, H), BF16),
    ("got_d", (HALVES, CHIPS, 16, H), BF16),
    ("mterm", (2, CHIPS, 16, C), BF16),
    ("mpair", (CHIPS, 16, C), BF16),
    ("msum", (CHIPS, 16, C), BF16),
    ("got_m", (CHIPS, 16, C), BF16),
    ("own", (2, CHIPS, 2, 8, 128), F32),
    ("opair", (CHIPS, 2, 8, 128), F32),
    ("ojoin", (CHIPS, 2, 8, 128), F32),
    ("got_own", (CHIPS, 2, 8, 128), F32),
    ("params", (2, CHIPS, 8, 128), F32),
    ("wdperm", (C, WIDE), BF16),
    ("wsperm", (WIDE, C), BF16),
    ("trail", (T + 8, C), F32),
    ("edge", (8, C), F32),
    ("late", (8, C), F32),
)
INPUTS = (
    ("inner", (T, C), BF16),
    ("gate", (T, C), BF16),
    ("grad", (T, C), BF16),
    ("taps", (TAPS, C), F32),
    ("shift", (1, C), F32),
    ("wsel", (PROJ, C), BF16),
    ("wdelta", (C, RANK), BF16),
    ("bias", (1, C), F32),
    ("dlog", (N, C), F32),
    ("skip", (1, C), F32),
)
OUTPUTS = (
    ("inner_grad", (T, C), BF16),
    ("gate_grad", (T, C), BF16),
    ("taps_grad", (TAPS, C), F32),
    ("shift_grad", (1, C), F32),
    ("select_grad", (17, C), F32),
    ("delta_grad", (16, C), F32),
    ("bias_grad", (1, C), F32),
    ("decay_grad", (N, C), F32),
    ("skip_grad", (1, C), F32),
)
SEMS = (
    ("in", (len(INPUTS),)),
    ("halo", (2,)),
    ("part", (2, TEN)),
    ("proj", (2, TEN)),
    ("ends", (2, CTX)),
    ("back", (2, CTX)),
    ("psel", (2, TEN)),
    ("sel", (2, TEN)),
    ("dpair", (HALVES, 2)),
    ("dsum", (HALVES, 2, CHIPS)),
    ("mpair", (2,)),
    ("msum", (2, CHIPS)),
    ("opair", (2,)),
    ("own", (2, CHIPS)),
    ("params", (2, CHIPS)),
    ("ppair", (2,)),
    ("edge", (2,)),
)


class Refs:
    pass


def tile_of(v, r, k):
    return v[8 * r : 8 * r + 8, 128 * k : 128 * k + 128]


def wide_of(v):
    return jnp.concatenate([v] * LT, 1)


def lane_sum(v):
    return functools.reduce(jnp.add, [v[:, 128 * k : 128 * k + 128] for k in range(LT)])


def half_lanes(h):
    return pl.ds(pl.multiple_of(h * H, H), H)


def convolve(z, first, rows):
    value = jnp.zeros((rows, C), F32) + z.shift[...]
    for k in range(TAPS):
        value = value + z.taps[k : k + 1, :] * z.pad[pl.ds(first + 16 - TAPS + 1 + k, rows), :]
    z.pre[pl.ds(first, rows), :] = value
    s = sigmoid(value)
    conv = value * s
    z.conv[pl.ds(first, rows), :] = conv
    z.half[pl.ds(first, rows), :] = conv.astype(BF16)
    z.slope[pl.ds(first, rows), :] = s * (1.0 + value * (1.0 - s))


def project(z, first, rows):
    half = z.half[pl.ds(first, rows), :]
    blocks = pl.ds(first // ROWS, rows // ROWS)
    shape = (rows // ROWS, ROWS)
    z.part[blocks, :, :RANK] = dot_nt(half, z.wsel[:RANK, :]).astype(BF16).reshape(*shape, RANK)
    z.part[blocks, :, RANK:] = split_tile(dot_nt(half, z.wtail[...])).reshape(*shape, 128)


def border_at(direction, r, k, h):
    return (direction * 8 + r * LT + k) * 2 + h


def summarize(z, h, lengths):
    lanes = slice(h * H, h * H + H)
    rate = jnp.exp(z.dlog[:, lanes]) * (-LOG2E)

    def steps(block, carried):
        state, decay, flow = carried
        for i in range(8):
            t = block * 8 + i
            row = pl.ds(t, 1)
            d = jnp.exp2(z.deltas[row, lanes] * rate)
            state = d * state + z.dx[row, lanes] * wide_of(z.bspread[t])
            decay = decay * d
            flow = flow + decay * (z.ocot[row, lanes] * wide_of(z.cspread[t]))
        return state, decay, flow

    zero = jnp.zeros((N, H), F32)
    state, _, flow = lax.fori_loop(0, T // 8, steps, (zero, zero + 1.0, zero))
    for r in range(N // 8):
        for k in range(LT):
            for direction, value in enumerate((state, flow)):
                at = border_at(direction, r, k, h)
                z.ends[at, 0:8, :] = tile_of(value, r, k)
                z.ends[at, 8:9, :] = lengths[:, h * H + 128 * k : h * H + 128 * k + 128]


def edges(z, direction, h):
    return jnp.concatenate(
        [
            jnp.concatenate([z.borders[border_at(direction, r, k, h)] for k in range(LT)], 1)
            for r in range(N // 8)
        ],
        0,
    )


class Fold:
    def __init__(self, rising):
        self.rising, self.waiting = rising, {}

    def push(self, value):
        value, step = value[0:8, :] + value[8:16, :], 1
        sub = iota(value.shape, 0)
        while step in self.waiting:
            other = self.waiting.pop(step)
            a, b = (other, value) if self.rising else (value, other)
            low = sub // step % 2 == 0
            value = jnp.where(low, a, b) + pltpu.roll(jnp.where(low, b, a), step, 0)
            step *= 2
        self.waiting[step] = value

    def result(self):
        return self.waiting[8]


def rows_of8(block):
    return pl.ds(pl.multiple_of(block * 8, 8), 8)


def go_forward(z, h):
    lanes = slice(h * H, h * H + H)
    rate2 = jnp.exp(z.dlog[:, lanes]) * (-LOG2E)

    def forward(block, state):
        y = Fold(True)
        for i in range(8):
            t = block * 8 + i
            row = pl.ds(t, 1)
            z.before[t] = state
            d = jnp.exp2(z.deltas[row, lanes] * rate2)
            state = d * state + z.dx[row, lanes] * wide_of(z.bspread[t])
            y.push(state * wide_of(z.cspread[t]))
            z.osum[h, t] = lane_sum(state * z.ocot[row, lanes])
        z.y[rows_of8(block), lanes] = y.result()
        return state

    lax.fori_loop(0, T // 8, forward, edges(z, 0, h))


def go_backward(z, h):
    lanes = slice(h * H, h * H + H)
    rate2 = jnp.exp(z.dlog[:, lanes]) * (-LOG2E)

    def backward(index, carried):
        flow, total = carried
        block = T // 8 - 1 - index
        along, wsum = Fold(False), Fold(False)
        for i in reversed(range(8)):
            t = block * 8 + i
            row = pl.ds(t, 1)
            delta = z.deltas[row, lanes]
            adjoint = z.ocot[row, lanes] * wide_of(z.cspread[t]) + flow
            z.isum[h, t] = lane_sum(adjoint * z.dx[row, lanes])
            along.push(adjoint * wide_of(z.bspread[t]))
            flow = jnp.exp2(delta * rate2) * adjoint
            weighted = flow * z.before[t]
            total = total + weighted * delta
            wsum.push(weighted * rate2)
        z.along[rows_of8(block), lanes] = along.result()
        z.wsum[rows_of8(block), lanes] = wsum.result() * (1.0 / LOG2E)
        return flow, total

    _, total = lax.fori_loop(0, T // 8, backward, (edges(z, 1, h), jnp.zeros((N, H), F32)))
    z.decay_part[:, lanes] = total * (rate2 * (1.0 / LOG2E))


def gather_sums(z):
    unit = jnp.ones((128, 128), BF16)
    place = iota((T * N, 128), 1) - iota((T * N, 128), 0) % N

    def summed(parts):
        return dot_nn((parts[0] + parts[1]).reshape(T * N, 128).astype(BF16), unit)

    both = jnp.where(
        place == 0, summed(z.isum), jnp.where(place == N, summed(z.osum), 0.0)
    ).astype(BF16)
    return dot_nn(z.fold[...], both)


def to_sibling(src, dst, sems):
    me = lax.axis_index("context")
    return pltpu.make_async_remote_copy(
        src_ref=src, dst_ref=dst, send_sem=sems.at[0], recv_sem=sems.at[1],
        device_id={"context": me + 1 - 2 * lax.rem(me, 2)}, device_id_type=MESH,
    )


def send_deltas(z, sem, h, pair):
    chip, core = lax.axis_index("context") // 2, lax.rem(lax.axis_index("context"), 2)
    pair.wait()
    z.dsum[h] = (z.dterm[h, core].astype(F32) + z.dpair[h].astype(F32)).astype(BF16)
    sent = Exchange(
        z.dsum.at[h], z.got_d.at[h], sem.dsum.at[h], "chips"
    )
    sent.start()
    z.got_d[h, chip] = z.dsum[h, chip]
    return sent


def layer_kernel(*refs):
    z, given, sem = Refs(), Refs(), Refs()
    refs = list(refs)
    for name, _, _ in INPUTS:
        setattr(given, name, refs.pop(0))
    for name, _, _ in OUTPUTS + INPUTS + SCRATCH:
        setattr(z, name, refs.pop(0))
    for name, _ in SEMS:
        setattr(sem, name, refs.pop(0))
    ctx, ten = lax.axis_index("context"), lax.axis_index("tensor")
    chip, core = ctx // 2, lax.rem(ctx, 2)

    greet("context")
    greet("tensor")
    loads = {}
    for i, (name, _, _) in enumerate(INPUTS):
        loads[name] = pltpu.make_async_copy(
            getattr(given, name), getattr(z, name), getattr(sem, "in").at[i]
        )

    for name in ("inner", "taps", "shift", "wsel", "gate", "grad", "dlog", "wdelta", "bias", "skip"):
        loads[name].start()

    for name in ("inner", "taps", "shift"):
        loads[name].wait()
    z.pad[16:, :] = z.inner[...].astype(F32)
    convolve(z, 16, T - 16)
    pl.semaphore_wait(pltpu.get_barrier_semaphore(), TEN - 1 + CTX - 1)
    halo = to_neighbour(z.inner.at[pl.ds(T - 16, 16)], z.halo, sem.halo.at[0], sem.halo.at[1], 1)
    halo.start()
    loads["wsel"].wait()
    tail = z.wsel[RANK:PROJ, :]
    z.wtail[0:32, :] = tail
    z.wtail[32:64, :] = jnp.zeros((32, C), BF16)
    z.wtail[64:96, :] = tail
    z.wtail[96:128, :] = jnp.zeros((32, C), BF16)
    project(z, 16, T - 16)
    halo.wait()
    z.pad[0:16, :] = z.halo[...].astype(F32) * (ctx > 0).astype(F32)
    convolve(z, 0, 16)
    project(z, 0, 16)
    scatter = Exchange(z.part, z.got_part, sem.part, "tensor")
    scatter.start()
    z.got_part[ten] = z.part[ten]

    loads["gate"].wait()
    loads["grad"].wait()
    g = z.gate[...].astype(F32)
    s = sigmoid(g)
    grad = z.grad[...].astype(F32)
    z.ocot[...] = grad * (g * s)
    z.gslope[...] = grad * (s * (1.0 + g * (1.0 - s)))

    scatter.wait_recv()
    total = jnp.sum(z.got_part[...].astype(F32), axis=0)
    bc = total[:, RANK:]
    bc = bc + pltpu.roll(bc, 64, 1)
    z.proj[ten, :, :RANK] = total[:, :RANK].astype(BF16)
    z.proj[ten, :, RANK:] = split_tile(bc)
    gather = Exchange(
        z.proj, z.proj, sem.proj, "tensor", same=True
    )
    gather.start()
    target = iota((WIDE, WIDE), 0)
    source = iota((WIDE, WIDE), 1)
    place = target % 256
    rest = target - RANK
    order = jnp.where(
        target < RANK,
        (place // 16 * 2 + target // 256) * 17 + place % 16,
        (rest % 16 * 2 + rest // 16) * 17 + 16,
    )
    order = ((order == source) & (target < PROJ)).astype(BF16)
    z.order[...] = order
    loads["wdelta"].wait()
    z.wdperm[...] = dot_nt(z.wdelta[...], order[:, :RANK]).astype(BF16)
    z.wsperm[...] = dot_nn(order[:, :PROJ], z.wsel[...]).astype(BF16)
    z.fold[...] = (iota((T, T * N), 0) == iota((T, T * N), 1) // N).astype(BF16)
    for name in ("dlog", "bias", "skip"):
        loads[name].wait()
    gather.wait_recv()

    flat = z.proj[...].reshape(T, WIDE)
    raw = dot_nt(flat[:, :RANK], z.wdelta[...]) + z.bias[...]
    step = jnp.maximum(raw, 0.0) + jnp.log1p(jnp.exp(-jnp.abs(raw)))
    z.deltas[...] = step
    lengths = jnp.sum(step, axis=0, keepdims=True)
    z.sig[...] = sigmoid(raw)
    z.dx[...] = step * z.conv[...]
    spread(z, flat[:, RANK:])
    ends = Exchange(z.ends, z.got_ends, sem.ends, "context")
    for h in range(HALVES):
        summarize(z, h, lengths)
        ends.to_core(h, lambda copy: copy.start())

    z.got_ends[ctx] = z.ends[ctx]
    backward = chip // 8
    at_row = pl.ds(pl.multiple_of(lax.rem(chip, 8) // LT * 8, 8), 8)
    at_lane = core * LT + lax.rem(chip, LT)
    rate = jnp.exp(z.dlog[at_row, pl.ds(pl.multiple_of(at_lane * 128, 128), 128)]) * (-LOG2E)
    ends.wait_recv()
    z.decays[...] = jnp.exp2(rate[None] * z.got_ends[:, 8:9, :])
    carried = jnp.zeros((8, 128), F32)
    for i in range(CTX):
        at = i + backward * (CTX - 1 - 2 * i)
        z.back[at] = carried
        carried = z.decays[at] * carried + z.got_ends[at, 0:8, :]
    home = Exchange(z.back, z.borders, sem.back, "context")
    home.start()
    z.borders[ctx] = z.back[ctx]
    scatter.wait_send()
    gather.wait_send()

    select_part = jnp.zeros((T, WIDE), F32)
    dpairs, deltas, sides = [], [], []
    for h in range(HALVES):
        lanes = slice(h * H, h * H + H)
        home.to_core(h, lambda copy: copy.wait_recv())
        go_forward(z, h)
        if h > 0:
            deltas.append(send_deltas(z, sem, h - 1, dpairs[h - 1]))
        go_backward(z, h)
        near = z.along[:, lanes]
        raw_cot = (z.wsum[:, lanes] + z.conv[:, lanes] * near) * z.sig[:, lanes]
        raw_half = raw_cot.astype(BF16)
        select_part = select_part + dot_nn(raw_half, z.wdperm[lanes, :])
        if h == HALVES - 1:
            select_part = select_part + dot_nt(gather_sums(z).astype(BF16), z.order[:, RANK:])
            z.psel[...] = select_part.astype(BF16).reshape(TEN, ROWS, WIDE)
            scatter2 = Exchange(z.psel, z.got_psel, sem.psel, "tensor")
            scatter2.start()
            z.got_psel[ten] = z.psel[ten]
        term = dot_tn(flat[:, :RANK], raw_half).astype(BF16).reshape(CHIPS, 2, 16, H)
        z.dterm[h, 0] = term[:, 0]
        z.dterm[h, 1] = term[:, 1]
        dpairs.append(to_sibling(z.dterm.at[h, 1 - core], z.dpair.at[h], sem.dpair.at[h]))
        dpairs[h].start()
        cot, gain, conv = z.ocot[:, lanes], z.skip[:, lanes], z.conv[:, lanes]
        z.gate_grad[:, lanes] = (
            z.gslope[:, lanes] * (z.y[:, lanes] + gain * conv)
        ).astype(BF16)
        z.direct[:, lanes] = gain * cot + z.deltas[:, lanes] * near
        sides.append(
            jnp.concatenate(
                [
                    jnp.sum(raw_cot, axis=0, keepdims=True),
                    jnp.sum(cot * conv, axis=0, keepdims=True),
                ],
                0,
            )
        )

    scatter2.wait_recv()
    z.sel[ten] = jnp.sum(z.got_psel[...].astype(F32), axis=0).astype(BF16)
    gather2 = Exchange(z.sel, z.sel, sem.sel, "tensor", same=True)
    gather2.start()
    deltas.append(send_deltas(z, sem, HALVES - 1, dpairs[HALVES - 1]))
    early = jnp.concatenate(sides, 1)
    for k in range(8):
        lanes = slice(128 * k, 128 * k + 128)
        z.own[0, k, 0] = z.decay_part[0:8, lanes]
        z.own[0, 8 + k, 0] = z.decay_part[8:16, lanes]
        z.own[1, 8 + k, 0] = jnp.zeros((8, 128), F32)
    gather2.wait_recv()
    select_cot = z.sel[...].reshape(T, WIDE)

    pre_cot = (z.direct[...] + dot_nn(select_cot, z.wsperm[...])) * z.slope[...]
    z.trail[0:T, :] = pre_cot
    z.edge[...] = pre_cot[0:8, :]
    below = to_neighbour(z.edge, z.late, sem.edge.at[0], sem.edge.at[1], -1)
    below.start()
    rows = [early, jnp.sum(pre_cot, axis=0, keepdims=True)]
    for k in range(TAPS):
        rows.append(
            jnp.sum(pre_cot * z.pad[pl.ds(16 - TAPS + 1 + k, T), :], axis=0, keepdims=True)
        )
    rows = jnp.concatenate(rows + [jnp.zeros((1, C), F32)], 0)
    extra = dot_tn(select_cot[:, RANK:], z.half[...])
    for k in range(8):
        lanes = slice(128 * k, 128 * k + 128)
        z.own[1, k, 0] = rows[:, lanes]
        z.own[0, :, 1, k, :] = extra[0:CHIPS, lanes]
        z.own[1, :, 1, k, :] = extra[CHIPS:CTX, lanes]
    opair = to_sibling(z.own.at[1 - core], z.opair, sem.opair)
    opair.start()

    z.mterm[...] = (
        dot_tn(select_cot[:, :RANK], z.half[...]).astype(BF16).reshape(2, CHIPS, 16, C)
    )
    mpair = to_sibling(z.mterm.at[1 - core], z.mpair, sem.mpair)
    mpair.start()
    opair.wait()
    z.ojoin[...] = z.own[core] + z.opair[...]
    sums = Exchange(z.ojoin, z.got_own, sem.own, "chips")
    sums.start()
    z.got_own[chip] = z.ojoin[chip]
    mpair.wait()
    z.msum[...] = (z.mterm[core].astype(F32) + z.mpair[...].astype(F32)).astype(BF16)
    mains = Exchange(z.msum, z.got_m, sem.msum, "chips")
    mains.start()
    z.got_m[chip] = z.msum[chip]

    below.wait()
    z.trail[T:, :] = z.late[...] * (ctx < CTX - 1).astype(F32)
    result = jnp.zeros((T, C), F32)
    for k in range(TAPS):
        result = result + z.taps[k : k + 1, :] * z.trail[pl.ds(TAPS - 1 - k, T), :]
    z.inner_grad[...] = result.astype(BF16)

    sums.wait_recv()
    z.params[core, chip] = jnp.sum(z.got_own[:, 0], axis=0)
    shares = Exchange(z.params.at[core], z.params.at[core], sem.params, "chips", same=True)
    shares.start()
    last = jnp.sum(z.got_own[:, 1], axis=0)
    for k in range(8):
        z.select_grad[16:17, 128 * k : 128 * k + 128] = last[k : k + 1, :]
    for h in range(HALVES):
        deltas[h].wait_recv()
        z.delta_grad[:, h * H : h * H + H] = jnp.sum(z.got_d[h].astype(F32), axis=0)
    for exchange in (ends, home, scatter2, gather2, deltas[0], deltas[1], sums):
        exchange.wait_send()
    shares.wait_recv()
    ppair = to_sibling(z.params.at[core], z.params.at[core], sem.ppair)
    ppair.start()
    mains.wait_recv()
    z.select_grad[0:16, :] = jnp.sum(z.got_m[...].astype(F32), axis=0)
    mains.wait_send()
    shares.wait_send()
    ppair.wait()
    for k in range(8):
        lanes = slice(128 * k, 128 * k + 128)
        z.decay_grad[0:8, lanes] = z.params[0, k]
        z.decay_grad[8:16, lanes] = z.params[0, 8 + k]
        rows = z.params[1, k]
        z.bias_grad[:, lanes] = rows[0:1, :]
        z.skip_grad[:, lanes] = rows[1:2, :]
        z.shift_grad[:, lanes] = rows[2:3, :]
        z.taps_grad[:, lanes] = rows[3:7, :]


def layer(*args):
    return pl.pallas_call(
        layer_kernel,
        out_shape=[jax.ShapeDtypeStruct(shape, kind) for _, shape, kind in OUTPUTS],
        in_specs=[pl.BlockSpec(memory_space=pl.ANY)] * len(INPUTS),
        out_specs=[VMEM] * len(OUTPUTS),
        scratch_shapes=[pltpu.VMEM(shape, kind) for _, shape, kind in INPUTS + SCRATCH]
        + [pltpu.SemaphoreType.DMA(shape) for _, shape in SEMS],
        compiler_params=pltpu.CompilerParams(
            collective_id=0, has_side_effects=True, vmem_limit_bytes=56 << 20
        ),
        name="layer",
    )(*args)


def finish_kernel(*refs):
    count = len(OUTPUTS)
    for given, out in zip(refs[:count], refs[count:]):
        out[...] = given[...]


def finish(*args):
    return pl.pallas_call(
        finish_kernel,
        out_shape=[jax.ShapeDtypeStruct(shape, kind) for _, shape, kind in OUTPUTS],
        in_specs=[VMEM] * len(OUTPUTS),
        out_specs=[VMEM] * len(OUTPUTS),
        name="finish",
    )(*args)


def body(
    inner_in, gate_in, out_grad, kernel, kernel_shift, select_proj, delta_proj, delta_bias,
    decay_log, skip_gain,
):
    parts = layer(
        inner_in, gate_in, out_grad, kernel.T, kernel_shift[None], select_proj, delta_proj,
        delta_bias[None], decay_log.T, skip_gain[None],
    )
    inner_grad, gate_grad, taps, shift, select, delta, bias, decay, skip = finish(*parts)
    return (
        inner_grad, gate_grad, taps.T, shift[0], select, delta.T, bias[0], decay.T, skip[0],
    )


def solution(mesh):
    return jax.shard_map(
        body,
        mesh=mesh,
        in_specs=(
            P("context", "tensor"),
            P("context", "tensor"),
            P("context", "tensor"),
            P("tensor", None),
            P("tensor"),
            P(None, "tensor"),
            P("tensor", None),
            P("tensor"),
            P("tensor", None),
            P("tensor"),
        ),
        out_specs=(
            P("context", "tensor"),
            P("context", "tensor"),
            P("tensor", None),
            P("tensor"),
            P("context", "tensor"),
            P("tensor", "context"),
            P("tensor"),
            P("tensor", None),
            P("tensor"),
        ),
        check_vma=False,
    )
```

time: 89 us -> 81.9 us (0.920)
  Pallas kernels: 88.2 us -> 81 us
    pallas_call x1, Pallas kernels: 86.2 us -> 79 us  [layer(): pl.pallas_call(layer_kernel, out_shape=[jax.ShapeDtypeStruct(shape, kind)...]
where the time goes in v4:
time: 81.9 us; the launch traced here: 81.8 us
  Pallas kernels  81 us (99%)
    pallas_call x1, Pallas kernels, layer(): pl.pallas_call(layer_kernel, out_shape=[jax.ShapeDtypeStruct(shape, kind)...  79 us
    pallas_call x1, Pallas kernels, finish(): pl.pallas_call(finish_kernel, out_shape=[jax.ShapeDtypeStruct(shape, kind...  2.08 us

profile of v4, /device:TPU:1, one launch (start us, length us, event | category | flops | bytes accessed | tf_op | source)
XLA Modules:
  0.0 81.8 jit_solution(10960822005540412492)
XLA Ops:
  0.6 79.0 %layer.1 = (bf16[128,1024]{1,0:T(8,128)(2,1)}, bf16[128,1024]{1,0:T(8,128)(2,1)}, f32[4,1024]{1,0:T(4,128)}, f32[1,1024]{1,0:T(1,128)}, f32[17,1024]{1,0:T(8,128...) custom-call(bf16[128,1024]{1,0:T(8,128)(2,1)} %refs_0_.1, ...), custom_call_target="tpu_custom_call" | custom-call | tf_op jit(solution)/shard_map/layer/pallas_call | solution.py:669
  79.6 2.1 %finish.1 = (bf16[128,1024]{1,0:T(8,128)(2,1)}, bf16[128,1024]{1,0:T(8,128)(2,1)}, f32[4,1024]{1,0:T(4,128)}, f32[1,1024]{1,0:T(1,128)}, f32[17,1024]{1,0:T(8,12...) custom-call(bf16[128,1024]{1,0:T(8,128)(2,1)} %get-tuple-element.27.refs_0_, ...), custom_call_target="tpu_custom_call" | custom-call | tf_op jit(solution)/shard_map/finish/pallas_call | solution.py:690

commit v5 on v4

--- a/solution.py
+++ b/solution.py
@@ -7,6 +7,7 @@
 from jax.experimental.pallas import tpu as pltpu
 from jax.sharding import PartitionSpec as P
 
+CONTEXT, TENSOR, CHIP = "context", "tensor", "chips"
 N = 16
 RANK = 512
 TAPS = 4
@@ -63,21 +64,21 @@
 
 
 def peer_of(group, k):
-    if group == "tensor":
-        at = lax.axis_index("tensor")
+    if group == TENSOR:
+        at = lax.axis_index(TENSOR)
         peer = lax.rem(at + far_first(k, TEN), TEN)
-        return at, peer, {"tensor": peer}
-    me = lax.axis_index("context")
-    place, core = (k // 2, 1 - k % 2) if group == "context" else (k, 0)
+        return at, peer, {TENSOR: peer}
+    me = lax.axis_index(CONTEXT)
+    place, core = (k // 2, 1 - k % 2) if group == CONTEXT else (k, 0)
     x = lax.rem(me // 8 + far_first(place // 4, 4), 4)
     y = lax.rem(me // 2 + far_first(place % 4, 4), 4)
     peer = (x * 4 + y) * 2 + lax.rem(me + core, 2)
-    if group == "chips":
-        return me // 2, x * 4 + y, {"context": peer}
-    return me, peer, {"context": peer}
-
-
-PEERS = {"tensor": TEN - 1, "context": CTX - 1, "chips": CHIPS - 1}
+    if group == CHIP:
+        return me // 2, x * 4 + y, {CONTEXT: peer}
+    return me, peer, {CONTEXT: peer}
+
+
+PEERS = {TENSOR: TEN - 1, CONTEXT: CTX - 1, CHIP: CHIPS - 1}
 
 
 class Exchange:
@@ -110,7 +111,7 @@
         self.every(lambda copy: copy.wait_send())
 
     def to_core(self, core, act):
-        other = lax.rem(lax.axis_index("context") + core, 2)
+        other = lax.rem(lax.axis_index(CONTEXT) + core, 2)
         lax.fori_loop(
             0, CHIPS - 1 + other, lambda q, _: (act(self.copy(2 * q + 1 - other)), 0)[1], 0
         )
@@ -124,10 +125,10 @@
 
 
 def to_neighbour(src, dst, send, recv, step):
-    peer = lax.rem(lax.axis_index("context") + step + CTX, CTX)
+    peer = lax.rem(lax.axis_index(CONTEXT) + step + CTX, CTX)
     return pltpu.make_async_remote_copy(
         src_ref=src, dst_ref=dst, send_sem=send, recv_sem=recv,
-        device_id={"context": peer}, device_id_type=MESH,
+        device_id={CONTEXT: peer}, device_id_type=MESH,
     )
 
 
@@ -184,15 +185,20 @@
     ("dpair", (HALVES, CHIPS, 16, H), BF16),
     ("dsum", (HALVES, CHIPS, 16, H), BF16),
     ("got_d", (HALVES, CHIPS, 16, H), BF16),
-    ("mterm", (2, CHIPS, 16, C), BF16),
-    ("mpair", (CHIPS, 16, C), BF16),
-    ("msum", (CHIPS, 16, C), BF16),
-    ("got_m", (CHIPS, 16, C), BF16),
-    ("own", (2, CHIPS, 2, 8, 128), F32),
-    ("opair", (CHIPS, 2, 8, 128), F32),
-    ("ojoin", (CHIPS, 2, 8, 128), F32),
-    ("got_own", (CHIPS, 2, 8, 128), F32),
+    ("mterm", (HALVES, 2, CHIPS, 16, H), BF16),
+    ("mpair", (HALVES, CHIPS, 16, H), BF16),
+    ("msum", (HALVES, CHIPS, 16, H), BF16),
+    ("got_m", (HALVES, CHIPS, 16, H), BF16),
+    ("early", (2, CHIPS, 8, 128), F32),
+    ("epair", (CHIPS, 8, 128), F32),
+    ("ejoin", (CHIPS, 8, 128), F32),
+    ("got_early", (CHIPS, 8, 128), F32),
     ("params", (2, CHIPS, 8, 128), F32),
+    ("own", (2, CHIPS, 16, 384), BF16),
+    ("opair", (CHIPS, 16, 384), BF16),
+    ("ojoin", (CHIPS, 16, 384), BF16),
+    ("got_own", (CHIPS, 16, 384), BF16),
+    ("late_sums", (2, 8, H), F32),
     ("wdperm", (C, WIDE), BF16),
     ("wsperm", (WIDE, C), BF16),
     ("trail", (T + 8, C), F32),
@@ -233,12 +239,15 @@
     ("sel", (2, TEN)),
     ("dpair", (HALVES, 2)),
     ("dsum", (HALVES, 2, CHIPS)),
-    ("mpair", (2,)),
-    ("msum", (2, CHIPS)),
+    ("mpair", (HALVES, 2)),
+    ("msum", (HALVES, 2, CHIPS)),
+    ("epair", (2,)),
+    ("early", (2, CHIPS)),
+    ("params", (2, CHIPS)),
+    ("ppair", (2,)),
     ("opair", (2,)),
     ("own", (2, CHIPS)),
-    ("params", (2, CHIPS)),
-    ("ppair", (2,)),
+    ("lpair", (2,)),
     ("edge", (2,)),
 )
 
@@ -406,22 +415,21 @@
 
 
 def to_sibling(src, dst, sems):
-    me = lax.axis_index("context")
+    me = lax.axis_index(CONTEXT)
     return pltpu.make_async_remote_copy(
         src_ref=src, dst_ref=dst, send_sem=sems.at[0], recv_sem=sems.at[1],
-        device_id={"context": me + 1 - 2 * lax.rem(me, 2)}, device_id_type=MESH,
+        device_id={CONTEXT: me + 1 - 2 * lax.rem(me, 2)}, device_id_type=MESH,
     )
 
 
-def send_deltas(z, sem, h, pair):
-    chip, core = lax.axis_index("context") // 2, lax.rem(lax.axis_index("context"), 2)
+def send_halves(z, sems, joined, own, other, got, h, pair):
+    chip, core = lax.axis_index(CONTEXT) // 2, lax.rem(lax.axis_index(CONTEXT), 2)
+    joined, own, other, got = (getattr(z, name) for name in (joined, own, other, got))
     pair.wait()
-    z.dsum[h] = (z.dterm[h, core].astype(F32) + z.dpair[h].astype(F32)).astype(BF16)
-    sent = Exchange(
-        z.dsum.at[h], z.got_d.at[h], sem.dsum.at[h], "chips"
-    )
+    joined[h] = (own[h, core].astype(F32) + other[h].astype(F32)).astype(BF16)
+    sent = Exchange(joined.at[h], got.at[h], sems.at[h], CHIP)
     sent.start()
-    z.got_d[h, chip] = z.dsum[h, chip]
+    got[h, chip] = joined[h, chip]
     return sent
 
 
@@ -434,11 +442,11 @@
         setattr(z, name, refs.pop(0))
     for name, _ in SEMS:
         setattr(sem, name, refs.pop(0))
-    ctx, ten = lax.axis_index("context"), lax.axis_index("tensor")
+    ctx, ten = lax.axis_index(CONTEXT), lax.axis_index(TENSOR)
     chip, core = ctx // 2, lax.rem(ctx, 2)
 
-    greet("context")
-    greet("tensor")
+    greet(CONTEXT)
+    greet(TENSOR)
     loads = {}
     for i, (name, _, _) in enumerate(INPUTS):
         loads[name] = pltpu.make_async_copy(
@@ -466,7 +474,7 @@
     z.pad[0:16, :] = z.halo[...].astype(F32) * (ctx > 0).astype(F32)
     convolve(z, 0, 16)
     project(z, 0, 16)
-    scatter = Exchange(z.part, z.got_part, sem.part, "tensor")
+    scatter = Exchange(z.part, z.got_part, sem.part, TENSOR)
     scatter.start()
     z.got_part[ten] = z.part[ten]
 
@@ -485,7 +493,7 @@
     z.proj[ten, :, :RANK] = total[:, :RANK].astype(BF16)
     z.proj[ten, :, RANK:] = split_tile(bc)
     gather = Exchange(
-        z.proj, z.proj, sem.proj, "tensor", same=True
+        z.proj, z.proj, sem.proj, TENSOR, same=True
     )
     gather.start()
     target = iota((WIDE, WIDE), 0)
@@ -515,7 +523,7 @@
     z.sig[...] = sigmoid(raw)
     z.dx[...] = step * z.conv[...]
     spread(z, flat[:, RANK:])
-    ends = Exchange(z.ends, z.got_ends, sem.ends, "context")
+    ends = Exchange(z.ends, z.got_ends, sem.ends, CONTEXT)
     for h in range(HALVES):
         summarize(z, h, lengths)
         ends.to_core(h, lambda copy: copy.start())
@@ -532,7 +540,7 @@
         at = i + backward * (CTX - 1 - 2 * i)
         z.back[at] = carried
         carried = z.decays[at] * carried + z.got_ends[at, 0:8, :]
-    home = Exchange(z.back, z.borders, sem.back, "context")
+    home = Exchange(z.back, z.borders, sem.back, CONTEXT)
     home.start()
     z.borders[ctx] = z.back[ctx]
     scatter.wait_send()
@@ -545,7 +553,9 @@
         home.to_core(h, lambda copy: copy.wait_recv())
         go_forward(z, h)
         if h > 0:
-            deltas.append(send_deltas(z, sem, h - 1, dpairs[h - 1]))
+            deltas.append(
+                send_halves(z, sem.dsum, "dsum", "dterm", "dpair", "got_d", h - 1, dpairs[h - 1])
+            )
         go_backward(z, h)
         near = z.along[:, lanes]
         raw_cot = (z.wsum[:, lanes] + z.conv[:, lanes] * near) * z.sig[:, lanes]
@@ -554,7 +564,7 @@
         if h == HALVES - 1:
             select_part = select_part + dot_nt(gather_sums(z).astype(BF16), z.order[:, RANK:])
             z.psel[...] = select_part.astype(BF16).reshape(TEN, ROWS, WIDE)
-            scatter2 = Exchange(z.psel, z.got_psel, sem.psel, "tensor")
+            scatter2 = Exchange(z.psel, z.got_psel, sem.psel, TENSOR)
             scatter2.start()
             z.got_psel[ten] = z.psel[ten]
         term = dot_tn(flat[:, :RANK], raw_half).astype(BF16).reshape(CHIPS, 2, 16, H)
@@ -577,19 +587,37 @@
             )
         )
 
+    for k in range(8):
+        lanes = slice(128 * k, 128 * k + 128)
+        z.early[0, k] = z.decay_part[0:8, lanes]
+        z.early[1, k] = z.decay_part[8:16, lanes]
+        z.early[:, 8 + k] = jnp.zeros((2, 8, 128), F32)
+    epair = to_sibling(z.early.at[1 - core], z.epair, sem.epair)
+    epair.start()
+    epair.wait()
+    z.ejoin[...] = z.early[core] + z.epair[...]
+    earlies = Exchange(z.ejoin, z.got_early, sem.early, CHIP)
+    earlies.start()
+    z.got_early[chip] = z.ejoin[chip]
     scatter2.wait_recv()
     z.sel[ten] = jnp.sum(z.got_psel[...].astype(F32), axis=0).astype(BF16)
-    gather2 = Exchange(z.sel, z.sel, sem.sel, "tensor", same=True)
+    gather2 = Exchange(z.sel, z.sel, sem.sel, TENSOR, same=True)
     gather2.start()
-    deltas.append(send_deltas(z, sem, HALVES - 1, dpairs[HALVES - 1]))
+    deltas.append(send_halves(z, sem.dsum, "dsum", "dterm", "dpair", "got_d", 1, dpairs[1]))
     early = jnp.concatenate(sides, 1)
-    for k in range(8):
-        lanes = slice(128 * k, 128 * k + 128)
-        z.own[0, k, 0] = z.decay_part[0:8, lanes]
-        z.own[0, 8 + k, 0] = z.decay_part[8:16, lanes]
-        z.own[1, 8 + k, 0] = jnp.zeros((8, 128), F32)
+    earlies.wait_recv()
+    z.params[core, chip] = jnp.sum(z.got_early[...], axis=0)
+    shares = Exchange(z.params.at[core], z.params.at[core], sem.params, CHIP, same=True)
+    shares.start()
     gather2.wait_recv()
     select_cot = z.sel[...].reshape(T, WIDE)
+
+    mpairs, mains = [], []
+    for h in range(HALVES):
+        term = dot_tn(select_cot[:, :RANK], z.half[:, h * H : h * H + H]).astype(BF16)
+        z.mterm[h] = term.reshape(2, CHIPS, 16, H)
+        mpairs.append(to_sibling(z.mterm.at[h, 1 - core], z.mpair.at[h], sem.mpair.at[h]))
+        mpairs[h].start()
 
     pre_cot = (z.direct[...] + dot_nn(select_cot, z.wsperm[...])) * z.slope[...]
     z.trail[0:T, :] = pre_cot
@@ -603,62 +631,63 @@
         )
     rows = jnp.concatenate(rows + [jnp.zeros((1, C), F32)], 0)
     extra = dot_tn(select_cot[:, RANK:], z.half[...])
-    for k in range(8):
-        lanes = slice(128 * k, 128 * k + 128)
-        z.own[1, k, 0] = rows[:, lanes]
-        z.own[0, :, 1, k, :] = extra[0:CHIPS, lanes]
-        z.own[1, :, 1, k, :] = extra[CHIPS:CTX, lanes]
+    for d in range(2):
+        mine = jnp.concatenate(
+            [rows[:, d * H : d * H + 256], rows[:, d * H + 256 : d * H + 512]], 0
+        ).astype(BF16)
+        for c in range(CHIPS):
+            row = extra[d * CHIPS + c : d * CHIPS + c + 1, :]
+            tile = jnp.concatenate(
+                [row[:, 128 * k : 128 * k + 128] for k in range(8)] + [jnp.zeros((8, 128), F32)], 0
+            )
+            z.own[d, c, :, 0:256] = mine
+            z.own[d, c, :, 256:384] = tile.astype(BF16)
     opair = to_sibling(z.own.at[1 - core], z.opair, sem.opair)
     opair.start()
-
-    z.mterm[...] = (
-        dot_tn(select_cot[:, :RANK], z.half[...]).astype(BF16).reshape(2, CHIPS, 16, C)
-    )
-    mpair = to_sibling(z.mterm.at[1 - core], z.mpair, sem.mpair)
-    mpair.start()
+    mains.append(send_halves(z, sem.msum, "msum", "mterm", "mpair", "got_m", 0, mpairs[0]))
     opair.wait()
-    z.ojoin[...] = z.own[core] + z.opair[...]
-    sums = Exchange(z.ojoin, z.got_own, sem.own, "chips")
+    z.ojoin[...] = (z.own[core].astype(F32) + z.opair[...].astype(F32)).astype(BF16)
+    sums = Exchange(z.ojoin, z.got_own, sem.own, CHIP)
     sums.start()
     z.got_own[chip] = z.ojoin[chip]
-    mpair.wait()
-    z.msum[...] = (z.mterm[core].astype(F32) + z.mpair[...].astype(F32)).astype(BF16)
-    mains = Exchange(z.msum, z.got_m, sem.msum, "chips")
-    mains.start()
-    z.got_m[chip] = z.msum[chip]
-
+    mains.append(send_halves(z, sem.msum, "msum", "mterm", "mpair", "got_m", 1, mpairs[1]))
+
+    shares.wait_recv()
+    ppair = to_sibling(z.params.at[core], z.params.at[core], sem.ppair)
+    ppair.start()
     below.wait()
     z.trail[T:, :] = z.late[...] * (ctx < CTX - 1).astype(F32)
     result = jnp.zeros((T, C), F32)
     for k in range(TAPS):
         result = result + z.taps[k : k + 1, :] * z.trail[pl.ds(TAPS - 1 - k, T), :]
     z.inner_grad[...] = result.astype(BF16)
-
-    sums.wait_recv()
-    z.params[core, chip] = jnp.sum(z.got_own[:, 0], axis=0)
-    shares = Exchange(z.params.at[core], z.params.at[core], sem.params, "chips", same=True)
-    shares.start()
-    last = jnp.sum(z.got_own[:, 1], axis=0)
-    for k in range(8):
-        z.select_grad[16:17, 128 * k : 128 * k + 128] = last[k : k + 1, :]
     for h in range(HALVES):
         deltas[h].wait_recv()
         z.delta_grad[:, h * H : h * H + H] = jnp.sum(z.got_d[h].astype(F32), axis=0)
-    for exchange in (ends, home, scatter2, gather2, deltas[0], deltas[1], sums):
-        exchange.wait_send()
-    shares.wait_recv()
-    ppair = to_sibling(z.params.at[core], z.params.at[core], sem.ppair)
-    ppair.start()
-    mains.wait_recv()
-    z.select_grad[0:16, :] = jnp.sum(z.got_m[...].astype(F32), axis=0)
-    mains.wait_send()
-    shares.wait_send()
     ppair.wait()
     for k in range(8):
         lanes = slice(128 * k, 128 * k + 128)
         z.decay_grad[0:8, lanes] = z.params[0, k]
-        z.decay_grad[8:16, lanes] = z.params[0, 8 + k]
-        rows = z.params[1, k]
+        z.decay_grad[8:16, lanes] = z.params[1, k]
+    for exchange in (ends, home, scatter2, gather2, deltas[0], deltas[1], earlies, shares):
+        exchange.wait_send()
+
+    sums.wait_recv()
+    both = jnp.sum(z.got_own[...].astype(F32), axis=0)
+    z.late_sums[core] = jnp.concatenate([both[0:8, 0:256], both[8:16, 0:256]], 1)
+    lpair = to_sibling(z.late_sums.at[core], z.late_sums.at[core], sem.lpair)
+    lpair.start()
+    for k in range(8):
+        z.select_grad[16:17, 128 * k : 128 * k + 128] = both[k : k + 1, 256:384]
+    for exchange in (sums, mains[0], mains[1]):
+        exchange.wait_send()
+    for h in range(HALVES):
+        mains[h].wait_recv()
+        z.select_grad[0:16, h * H : h * H + H] = jnp.sum(z.got_m[h].astype(F32), axis=0)
+    lpair.wait()
+    for d in range(2):
+        lanes = slice(d * H, d * H + H)
+        rows = z.late_sums[d]
         z.bias_grad[:, lanes] = rows[0:1, :]
         z.skip_grad[:, lanes] = rows[1:2, :]
         z.shift_grad[:, lanes] = rows[2:3, :]
@@ -715,27 +744,27 @@
         body,
         mesh=mesh,
         in_specs=(
-            P("context", "tensor"),
-            P("context", "tensor"),
-            P("context", "tensor"),
-            P("tensor", None),
-            P("tensor"),
-            P(None, "tensor"),
-            P("tensor", None),
-            P("tensor"),
-            P("tensor", None),
-            P("tensor"),
+            P(CONTEXT, TENSOR),
+            P(CONTEXT, TENSOR),
+            P(CONTEXT, TENSOR),
+            P(TENSOR, None),
+            P(TENSOR),
+            P(None, TENSOR),
+            P(TENSOR, None),
+            P(TENSOR),
+            P(TENSOR, None),
+            P(TENSOR),
         ),
         out_specs=(
-            P("context", "tensor"),
-            P("context", "tensor"),
-            P("tensor", None),
-            P("tensor"),
-            P("context", "tensor"),
-            P("tensor", "context"),
-            P("tensor"),
-            P("tensor", None),
-            P("tensor"),
+            P(CONTEXT, TENSOR),
+            P(CONTEXT, TENSOR),
+            P(TENSOR, None),
+            P(TENSOR),
+            P(CONTEXT, TENSOR),
+            P(TENSOR, CONTEXT),
+            P(TENSOR),
+            P(TENSOR, None),
+            P(TENSOR),
         ),
         check_vma=False,
     )

time: 81.9 us -> 79.7 us (0.973)
  Pallas kernels: 81 us -> 78.8 us
    pallas_call x1, Pallas kernels: 79 us -> 76.7 us  [layer(): pl.pallas_call(layer_kernel, out_shape=[jax.ShapeDtypeStruct(shape, kind)...]
where the time goes in v5:
time: 79.7 us; the launch traced here: 79.6 us
  Pallas kernels  78.8 us (99%)
    pallas_call x1, Pallas kernels, layer(): pl.pallas_call(layer_kernel, out_shape=[jax.ShapeDtypeStruct(shape, kind)...  76.7 us
    pallas_call x1, Pallas kernels, finish(): pl.pallas_call(finish_kernel, out_shape=[jax.ShapeDtypeStruct(shape, kind...  2.08 us

profile of v5, /device:TPU:1, one launch (start us, length us, event | category | flops | bytes accessed | tf_op | source)
XLA Modules:
  0.0 79.6 jit_solution(11110149061741906622)
XLA Ops:
  0.6 76.7 %layer.1 = (bf16[128,1024]{1,0:T(8,128)(2,1)}, bf16[128,1024]{1,0:T(8,128)(2,1)}, f32[4,1024]{1,0:T(4,128)}, f32[1,1024]{1,0:T(1,128)}, f32[17,1024]{1,0:T(8,128...) custom-call(bf16[128,1024]{1,0:T(8,128)(2,1)} %refs_0_.1, ...), custom_call_target="tpu_custom_call" | custom-call | tf_op jit(solution)/shard_map/layer/pallas_call | solution.py:698
  77.4 2.1 %finish.1 = (bf16[128,1024]{1,0:T(8,128)(2,1)}, bf16[128,1024]{1,0:T(8,128)(2,1)}, f32[4,1024]{1,0:T(4,128)}, f32[1,1024]{1,0:T(1,128)}, f32[17,1024]{1,0:T(8,12...) custom-call(bf16[128,1024]{1,0:T(8,128)(2,1)} %get-tuple-element.27.refs_0_, ...), custom_call_target="tpu_custom_call" | custom-call | tf_op jit(solution)/shard_map/finish/pallas_call | solution.py:719

commit v6 on v5

--- a/solution.py
+++ b/solution.py
@@ -594,6 +594,7 @@
         z.early[:, 8 + k] = jnp.zeros((2, 8, 128), F32)
     epair = to_sibling(z.early.at[1 - core], z.epair, sem.epair)
     epair.start()
+    deltas.append(send_halves(z, sem.dsum, "dsum", "dterm", "dpair", "got_d", 1, dpairs[1]))
     epair.wait()
     z.ejoin[...] = z.early[core] + z.epair[...]
     earlies = Exchange(z.ejoin, z.got_early, sem.early, CHIP)
@@ -603,7 +604,6 @@
     z.sel[ten] = jnp.sum(z.got_psel[...].astype(F32), axis=0).astype(BF16)
     gather2 = Exchange(z.sel, z.sel, sem.sel, TENSOR, same=True)
     gather2.start()
-    deltas.append(send_halves(z, sem.dsum, "dsum", "dterm", "dpair", "got_d", 1, dpairs[1]))
     early = jnp.concatenate(sides, 1)
     earlies.wait_recv()
     z.params[core, chip] = jnp.sum(z.got_early[...], axis=0)

time: 79.7 us -> 79.7 us (level)
  no operation moved by 1% of the time
where the time goes in v6:
time: 79.7 us; the launch traced here: 79.6 us
  Pallas kernels  78.8 us (99%)
    pallas_call x1, Pallas kernels, layer(): pl.pallas_call(layer_kernel, out_shape=[jax.ShapeDtypeStruct(shape, kind)...  76.7 us
    pallas_call x1, Pallas kernels, finish(): pl.pallas_call(finish_kernel, out_shape=[jax.ShapeDtypeStruct(shape, kind...  2.08 us

profile of v6, /device:TPU:1, one launch (start us, length us, event | category | flops | bytes accessed | tf_op | source)
XLA Modules:
  0.0 79.6 jit_solution(13071321785224195560)
XLA Ops:
  0.6 76.7 %layer.1 = (bf16[128,1024]{1,0:T(8,128)(2,1)}, bf16[128,1024]{1,0:T(8,128)(2,1)}, f32[4,1024]{1,0:T(4,128)}, f32[1,1024]{1,0:T(1,128)}, f32[17,1024]{1,0:T(8,128...) custom-call(bf16[128,1024]{1,0:T(8,128)(2,1)} %refs_0_.1, ...), custom_call_target="tpu_custom_call" | custom-call | tf_op jit(solution)/shard_map/layer/pallas_call | solution.py:698
  77.4 2.1 %finish.1 = (bf16[128,1024]{1,0:T(8,128)(2,1)}, bf16[128,1024]{1,0:T(8,128)(2,1)}, f32[4,1024]{1,0:T(4,128)}, f32[1,1024]{1,0:T(1,128)}, f32[17,1024]{1,0:T(8,12...) custom-call(bf16[128,1024]{1,0:T(8,128)(2,1)} %get-tuple-element.27.refs_0_, ...), custom_call_target="tpu_custom_call" | custom-call | tf_op jit(solution)/shard_map/finish/pallas_call | solution.py:719
